TPU v7x, 512 devices: a whole 4x8x8 slice. The times are simulated.
512 devices in a mesh: pts: 512 (over x, y, z, core).
Axes of the slice: x: 4, y: 8, z: 8, core: 2. Of those that a mesh axis runs over, the one named last changes fastest.
Arguments:
- points: bfloat16 [262144, 256], P('pts'), may hold values from -24 to 24
- patch_ids: int32 [262144], P('pts'), may hold values from 0 to 639, never falling along the last dimension, each value on 1 to 512 neighbouring positions
- cell_ids: int32 [262144], P('pts'), may hold values from 0 to 65535, as said below
- norm_gain: float32 [256], replicated, may hold values from 0.8 to 2
- w_qkv: bfloat16 [256, 768], replicated, may hold values from -0.375 to 0.375
- w_out: bfloat16 [256, 256], replicated, may hold values from -0.375 to 0.375
- w_pool: bfloat16 [256, 512], replicated, may hold values from -0.375 to 0.375
- b_pool: float32 [512], replicated, may hold values from -4 to 4
- pool_gain: float32 [512], replicated, may hold values from 0.5 to 1.5
- cotangent: float32 [65536, 512], P('pts'), may hold values from -6 to 6
Outputs:
- grad_points: float32 [262144, 256], P('pts')
- grad_qkv: float32 [256, 768], replicated
- grad_w_out: float32 [256, 256], replicated
- grad_norm_gain: float32 [256], replicated
- grad_w_pool: float32 [256, 512], replicated
- grad_b_pool: float32 [512], replicated
- grad_pool_gain: float32 [512], replicated
Inputs may be any that keep to these rules, and one draw needn't show every extreme that they name: `patch_ids`: patch ids never fall; every patch has 1 to 512 points and some patch has exactly 512. `cell_ids`: cell ids never fall and every cell has a point; point 0 is in cell 0; points d * 512 to (d + 1) * 512 - 1 hold the first points of exactly the cells d * 128 to (d + 1) * 128 - 1, for d above 0 none of them among the first 128 points of that range, so for d above 0 those first points belong to cell d * 128 - 1.
All inputs are finite; a program needn't handle non-finite values.
Results may differ from a plain program's by a relative error of at most 0.024.
Values may be sent and summed in bfloat16 or wider, within the bound.
A program may use at most 64 MiB of HBM per device.

v0:
```python
import functools
import math

import jax
import jax.numpy as jnp
from jax import lax
from jax.experimental import pallas as pl
from jax.experimental.pallas import tpu as pltpu
from jax.sharding import PartitionSpec as P

PATCH = 512
MESH = pl.DeviceIdType.MESH


EPS = 1e-05
ROOT_HALF = 0.7071067811865476
ROOT_TWO_PI = 2.5066282746310002


def layer_stats(values):
    centered = values - jnp.mean(values, axis=-1, keepdims=True)
    inv_std = lax.rsqrt(jnp.mean(centered * centered, axis=-1, keepdims=True) + EPS)
    return (centered * inv_std, inv_std)


def norm_back(grad_normed, normed, inv_std):
    first_mean = jnp.mean(grad_normed, axis=-1, keepdims=True)
    second_mean = jnp.mean(grad_normed * normed, axis=-1, keepdims=True)
    return inv_std * (grad_normed - first_mean - normed * second_mean)


def gelu_slope(scaled):
    normal_cdf = 0.5 * (1.0 + lax.erf(scaled * ROOT_HALF))
    return normal_cdf + scaled * jnp.exp(-0.5 * scaled * scaled) / ROOT_TWO_PI


def inner_rows(left, right):
    return lax.dot_general(
        left, right, (((0,), (0,)), ((), ())), preferred_element_type=jnp.float32
    )


def against_rows(left, right):
    return lax.dot_general(
        left, right, (((1,), (1,)), ((), ())), preferred_element_type=jnp.float32
    )


HALF = 128
PER_HALF = 8
HEAD_SIZE = 16
TILE = 128
CHUNK = 528
TALL = 3 * CHUNK
TILES = PATCH // TILE
PAIR = 256 // TILE
WINDOW = 3 * PATCH
FAR = float(2**30)
DIGIT = 32
LOG_LANE = 64


def head_mask(h, axis):
    shape = (1, 2 * HALF) if axis else (2 * HALF, 1)
    place = lax.broadcasted_iota(jnp.int32, shape, axis)
    own = (place >= h * HEAD_SIZE) & (place < (h + 1) * HEAD_SIZE)
    marks = (place >= HALF) & (place < HALF + LOG_LANE)
    terms = (place >= HALF + LOG_LANE) & (place < HALF + LOG_LANE + 24) & (place % PER_HALF == h)
    return (own | marks | terms).astype(jnp.float32).astype(jnp.bfloat16)


def split_three(values, which):
    first = values.astype(jnp.bfloat16).astype(jnp.float32)
    second = (values - first).astype(jnp.bfloat16).astype(jnp.float32)
    third = values - first - second
    return jnp.where(which == 0, first, jnp.where(which == 1, second, third))


def neighbours():
    me = lax.axis_index("pts")
    count = lax.axis_size("pts")
    return me, (me + count - 1) % count, (me + 1) % count


def greet_neighbours(before, after):
    barrier = pltpu.get_barrier_semaphore()
    for device in (before, after):
        pl.semaphore_signal(barrier, inc=1, device_id=(device,), device_id_type=MESH)
    pl.semaphore_wait(barrier, 2)


def send(source, landing, sems, index, device):
    copy = pltpu.make_async_remote_copy(
        src_ref=source,
        dst_ref=landing,
        send_sem=sems.at[0, index],
        recv_sem=sems.at[1, index],
        device_id=(device,),
        device_id_type=MESH,
    )
    copy.start()
    return copy


def digit_columns(marks):
    row = lax.broadcasted_iota(jnp.int32, (HALF, HALF), 0)
    high, low = marks // DIGIT, marks % DIGIT
    hit = ((row < DIGIT) & (row == high)) | ((row >= DIGIT) & (row < LOG_LANE) & (row - DIGIT == low))
    return hit.astype(jnp.float32)


def prepare_kernel(
    points_hbm, ids_hbm, gain_hbm, w_hbm, q_ref, qt_ref, kg_ref, vg_ref, f_ref, hidden_ref, spans_ref,
    points, ids, gain, w_qkv, marks, marks_low, marks_high, rows_low, rows_high, sems, local_sems,
):
    me, before, after = neighbours()
    local = []
    for i, (source, target) in enumerate(
        ((ids_hbm, ids), (points_hbm, points), (w_hbm, w_qkv), (gain_hbm, gain))
    ):
        local.append(pltpu.make_async_copy(source, target, local_sems.at[i]))
        local[-1].start()
    marks[...] = jnp.zeros_like(marks)
    greet_neighbours(before, after)
    local[0].wait()
    marks[:4, :] = ids[...] + 1
    local[1].wait()
    copies = [
        send(points, rows_high, sems, 0, before),
        send(points, rows_low, sems, 1, after),
        send(marks, marks_high, sems, 2, before),
        send(marks, marks_low, sems, 3, after),
    ]
    local[2].wait()
    local[3].wait()

    def project(block, first, columns):
        normed, _ = layer_stats(block[...].astype(jnp.float32))
        hidden = (normed * gain[...]).astype(jnp.bfloat16)
        hidden_ref[first : first + PATCH, :] = hidden
        return jnp.dot(hidden, w_qkv[:, columns], preferred_element_type=jnp.float32)

    def place(first, keys, values):
        for g in range(2):
            lanes = slice(g * HALF, (g + 1) * HALF)
            kg_ref[g, first : first + PATCH, :HALF] = keys[:, lanes].astype(jnp.bfloat16)
            vg_ref[g, first : first + PATCH, :HALF] = values[:, lanes].astype(jnp.bfloat16)

    def place_marks(block, first, own):
        lane = lax.broadcasted_iota(jnp.int32, (HALF, HALF), 1)
        row = lax.broadcasted_iota(jnp.int32, (HALF, HALF), 0)
        terms = (lane >= LOG_LANE) & (lane < LOG_LANE + 24)
        for i in range(4):
            rows = slice(first + i * HALF, first + (i + 1) * HALF)
            digits = digit_columns(block[i : i + 1, :])
            both = jnp.where(terms, 1.0, digits.T).astype(jnp.bfloat16)
            for g in range(2):
                kg_ref[g, rows, HALF:] = both
                vg_ref[g, rows, HALF:] = both
            if own:
                away = jnp.where(row < LOG_LANE, (1.0 - digits) * -FAR, 0.0)
                f_ref[:, i * HALF : (i + 1) * HALF] = away.astype(jnp.bfloat16)

    qkv = project(points, PATCH, slice(None))
    queries = qkv[:, :256].astype(jnp.bfloat16).astype(jnp.float32) * 0.25
    q_ref[...] = queries.astype(jnp.bfloat16)
    qt_ref[...] = queries.T.astype(jnp.bfloat16)
    place(PATCH, qkv[:, 256:512], qkv[:, 512:])
    own = marks[...]
    place_marks(own, PATCH, True)
    lane = lax.broadcasted_iota(jnp.int32, (TALL - WINDOW, 2 * HALF), 1)
    nowhere = ((lane == HALF) | (lane == HALF + DIGIT)).astype(jnp.float32).astype(jnp.bfloat16)
    for g in range(2):
        kg_ref[g, WINDOW:, :] = nowhere
        vg_ref[g, WINDOW:, :] = nowhere
    for copy in copies[2:]:
        copy.wait()
    low = jnp.where(me == 0, 0, marks_low[...])
    high = jnp.where(me == lax.axis_size("pts") - 1, 0, marks_high[...])
    place_marks(low, 0, False)
    place_marks(high, 2 * PATCH, False)
    own_f, low_f, high_f = (block[:4].astype(jnp.float32) for block in (own, low, high))
    for t in range(TILES):
        ours = own_f[t * TILE // HALF : (t + 1) * TILE // HALF]
        first, last = jnp.min(ours), jnp.max(ours)
        lower = jnp.sum((low_f < first).astype(jnp.float32) + (own_f < first).astype(jnp.float32))
        upper = jnp.sum(
            ((high_f > 0) & (high_f <= last)).astype(jnp.float32) + (own_f <= last).astype(jnp.float32)
        )
        lower = lower.astype(jnp.int32) // 16 * 16
        count = (PATCH + upper.astype(jnp.int32) - lower + CHUNK - 1) // CHUNK
        spans_ref[t, 0] = jnp.minimum(lower, TALL - count * CHUNK)
        spans_ref[t, 1] = count
    for copy, block, first in ((copies[1], rows_low, 0), (copies[0], rows_high, 2 * PATCH)):
        copy.wait()
        kv = project(block, first, slice(256, 768))
        place(first, kv[:, :256], kv[:, 256:])


def prepare(points, ids, gain, w_qkv):
    half = jnp.bfloat16
    vmem = pl.BlockSpec(memory_space=pltpu.VMEM)
    return pl.pallas_call(
        prepare_kernel,
        out_shape=[
            jax.ShapeDtypeStruct((PATCH, 256), half),
            jax.ShapeDtypeStruct((256, PATCH), half),
            jax.ShapeDtypeStruct((2, TALL, 2 * HALF), half),
            jax.ShapeDtypeStruct((2, TALL, 2 * HALF), half),
            jax.ShapeDtypeStruct((HALF, PATCH), half),
            jax.ShapeDtypeStruct((WINDOW, 256), half),
            jax.ShapeDtypeStruct((TILES, 2), jnp.int32),
        ],
        in_specs=[pl.BlockSpec(memory_space=pl.ANY)] * 4,
        out_specs=[vmem] * 6 + [pl.BlockSpec(memory_space=pltpu.SMEM)],
        scratch_shapes=[
            pltpu.VMEM((PATCH, 256), half),
            pltpu.VMEM((4, HALF), jnp.int32),
            pltpu.VMEM((1, 256), jnp.float32),
            pltpu.VMEM((256, 768), half),
            pltpu.VMEM((8, HALF), jnp.int32),
            pltpu.VMEM((8, HALF), jnp.int32),
            pltpu.VMEM((8, HALF), jnp.int32),
            pltpu.VMEM((PATCH, 256), half),
            pltpu.VMEM((PATCH, 256), half),
            pltpu.SemaphoreType.DMA((2, 4)),
            pltpu.SemaphoreType.DMA((4,)),
        ],
        compiler_params=pltpu.CompilerParams(
            collective_id=1, has_side_effects=True, vmem_limit_bytes=32 * 1024 * 1024
        ),
        name="prepare",
    )(points, ids, gain, w_qkv)


SLOTS = 144


def membership(cells):
    local = cells - lax.axis_index("pts") * HALF
    local = jnp.where(local < 0, HALF, local)
    slot = lax.broadcasted_iota(jnp.int32, (SLOTS, HALF), 0)
    parts = [(slot == local[i : i + 1, :]).astype(jnp.float32) for i in range(4)]
    return jnp.concatenate(parts, axis=1)


def tall_max(scores):
    part = CHUNK // 6
    folded = scores[:part]
    for i in range(1, 6):
        folded = jnp.maximum(folded, scores[i * part : (i + 1) * part])
    return jnp.max(folded, axis=0, keepdims=True)


def forward_kernel(
    spans, qt_ref, f_ref, kg_ref, vg_ref, points_hbm, w_out_hbm, cells_hbm,
    att_ref, logs_ref, sums_ref, counts_ref, qt, kept, att_t, top_t, total_t, points, w_out, cells, sems,
):
    tile, half = pl.program_id(0), pl.program_id(1)
    start, count = spans[tile, 0], spans[tile, 1]
    late = [
        pltpu.make_async_copy(source, target, sems.at[i])
        for i, (source, target) in enumerate(
            ((points_hbm, points), (w_out_hbm, w_out), (cells_hbm, cells))
        )
    ]

    @pl.when((tile == 0) & (half == 0))
    def _():
        for copy in late:
            copy.start()

    both = jnp.concatenate([qt_ref[...], f_ref[...]], axis=0)
    for h in range(PER_HALF):
        qt[h // PAIR, :, h % PAIR * TILE : (h % PAIR + 1) * TILE] = both * head_mask(h, 0)
    top_t[...] = jnp.full_like(top_t, -3e38)
    total_t[...] = jnp.zeros_like(total_t)
    att_t[...] = jnp.zeros_like(att_t)

    def chunk(c, carry):
        rows = pl.ds(pl.multiple_of(start + c * CHUNK, 16), CHUNK)
        values_t = vg_ref[half, rows, :HALF].astype(jnp.float32).T.astype(jnp.bfloat16)
        ones = jnp.ones((16, CHUNK), jnp.bfloat16)
        tops = []
        for p in range(PER_HALF // PAIR):
            scores = jnp.dot(kg_ref[half, rows, :], qt[p], preferred_element_type=jnp.float32)
            kept[p] = scores
            tops.append(jnp.maximum(top_t[p : p + 1, :], tall_max(scores)))
        for p in range(PER_HALF // PAIR):
            before, top = top_t[p : p + 1, :], tops[p]
            weights = jnp.exp(kept[p] - top).astype(jnp.bfloat16)
            decay = jnp.exp(before - top)
            top_t[p : p + 1, :] = top
            own = slice(p * PAIR * HEAD_SIZE, (p + 1) * PAIR * HEAD_SIZE)
            left = jnp.concatenate([values_t[own], ones], axis=0)
            mixed = jnp.dot(left, weights, preferred_element_type=jnp.float32)
            count_rows = PAIR * HEAD_SIZE
            total_t[p : p + 1, :] = total_t[p : p + 1, :] * decay + mixed[count_rows : count_rows + 1]
            att_t[own, :] = att_t[own, :] * decay + mixed[:count_rows]
        return carry

    lax.fori_loop(0, count, chunk, 0)
    rows = pl.ds(pl.multiple_of(tile * TILE, TILE), TILE)
    logs_p = -(top_t[...] + jnp.log(total_t[...]))
    parts, logs = [], []
    for h in range(PER_HALF):
        p, columns = h // PAIR, slice(h % PAIR * TILE, (h % PAIR + 1) * TILE)
        mine = att_t[h * HEAD_SIZE : (h + 1) * HEAD_SIZE, columns]
        parts.append(mine / total_t[p : p + 1, columns])
        logs.append(logs_p[p : p + 1, columns])
    attended = jnp.concatenate(parts, axis=0).T.astype(jnp.bfloat16)
    for g in range(2):

        @pl.when(half == g)
        def _():
            att_ref[rows, g * HALF : (g + 1) * HALF] = attended

    logs = jnp.concatenate(logs, axis=0)
    terms = [split_three(logs, i) for i in range(3)]
    logs_ref[:LOG_LANE, :] = f_ref[:LOG_LANE, :]
    spare = jnp.zeros((HALF - LOG_LANE - 24, TILE), jnp.float32)
    logs_ref[LOG_LANE:, :] = jnp.concatenate(terms + [spare], axis=0).astype(jnp.bfloat16)

    @pl.when((tile == TILES - 1) & (half == 1))
    def _():
        for copy in late:
            copy.wait()
        mixed = points[...].astype(jnp.float32) + jnp.dot(
            att_ref[...], w_out[...], preferred_element_type=jnp.float32
        )
        member = membership(cells[...])
        sums_ref[...] = jnp.dot(
            member.astype(jnp.bfloat16), mixed.astype(jnp.bfloat16), preferred_element_type=jnp.float32
        )
        counts_ref[...] = jnp.broadcast_to(jnp.sum(member, axis=1, keepdims=True), (SLOTS, HALF))


def attend(spans, queries_t, marks_f, keys_g, values_g, points, w_out, cells):
    def whole(*shape):
        return pl.BlockSpec(shape, lambda t, g: (0,) * len(shape))

    outside = pl.BlockSpec(memory_space=pl.ANY)
    return pl.pallas_call(
        forward_kernel,
        grid=(TILES, 2),
        out_shape=[
            jax.ShapeDtypeStruct((PATCH, 256), jnp.bfloat16),
            jax.ShapeDtypeStruct((256, PATCH), jnp.bfloat16),
            jax.ShapeDtypeStruct((SLOTS, 256), jnp.float32),
            jax.ShapeDtypeStruct((SLOTS, HALF), jnp.float32),
        ],
        in_specs=[
            pl.BlockSpec(memory_space=pltpu.SMEM),
            pl.BlockSpec((HALF, TILE), lambda t, g: (g, t)),
            pl.BlockSpec((HALF, TILE), lambda t, g: (0, t)),
            whole(2, TALL, 2 * HALF),
            whole(2, TALL, 2 * HALF),
            outside,
            outside,
            outside,
        ],
        out_specs=[
            whole(PATCH, 256),
            pl.BlockSpec((HALF, TILE), lambda t, g: (g, t)),
            whole(SLOTS, 256),
            whole(SLOTS, HALF),
        ],
        scratch_shapes=[
            pltpu.VMEM((PER_HALF // PAIR, 2 * HALF, PAIR * TILE), jnp.bfloat16),
            pltpu.VMEM((PER_HALF // PAIR, CHUNK, PAIR * TILE), jnp.float32),
            pltpu.VMEM((HALF, PAIR * TILE), jnp.float32),
            pltpu.VMEM((PER_HALF // PAIR, PAIR * TILE), jnp.float32),
            pltpu.VMEM((PER_HALF // PAIR, PAIR * TILE), jnp.float32),
            pltpu.VMEM((PATCH, 256), jnp.bfloat16),
            pltpu.VMEM((256, 256), jnp.bfloat16),
            pltpu.VMEM((4, HALF), jnp.int32),
            pltpu.SemaphoreType.DMA((3,)),
        ],
        compiler_params=pltpu.CompilerParams(vmem_limit_bytes=40 * 1024 * 1024),
        name="attention",
    )(spans, queries_t, marks_f, keys_g, values_g, points, w_out, cells)


def pool_kernel(
    scale, sums, counts, cells, att, w_out, w_pool, b_pool, pool_gain, cotangent,
    dmixed_ref, datt_ref, datt_t_ref, delta_ref, gw_pool, gw_out, gb_pool, g_gain,
    back_pack, ahead_pack, from_after, from_before, sems,
):
    me, before, after = neighbours()
    back_pack[:, :256] = sums[HALF : HALF + 8, :]
    back_pack[:, 256:] = counts[HALF : HALF + 8, :]
    ahead_pack[:, :256] = sums[HALF - 8 : HALF, :]
    ahead_pack[:, 256:384] = counts[HALF - 8 : HALF, :]
    ahead_pack[:, 384:] = cotangent[HALF - 8 :, :]
    greet_neighbours(before, after)
    copies = [
        send(back_pack, from_after, sems, 0, before),
        send(ahead_pack, from_before, sems, 1, after),
    ]
    member = membership(cells[...]).astype(jnp.bfloat16)
    for copy in copies:
        copy.wait()
    row = lax.broadcasted_iota(jnp.int32, (8, 1), 0)
    late, early = from_after[0:1, :], from_before[7:8, :]
    last_sum = sums[HALF - 8 : HALF, :] + jnp.where(row == 7, late[:, :256], 0.0)
    lead_sum = jnp.where(row == 0, sums[HALF : HALF + 8, :] + early[:, :256], 0.0)
    last_count = counts[HALF - 8 : HALF, :] + jnp.where(row == 7, late[:, 256:], 0.0)
    lead_count = jnp.where(row == 0, counts[HALF : HALF + 8, :] + early[:, 256:384], 0.0)
    spare = jnp.zeros((8, 256), jnp.float32)
    all_sums = jnp.concatenate([sums[: HALF - 8, :], last_sum, lead_sum, spare], axis=0)
    all_counts = jnp.concatenate(
        [counts[: HALF - 8, :], last_count, lead_count, spare[:, :HALF]], axis=0
    )[:, :1]
    all_counts = jnp.maximum(all_counts, 1.0)
    lead_cot = jnp.where(row == 0, early[:, 384:], 0.0)
    all_cot = jnp.concatenate([cotangent[...], lead_cot, jnp.zeros((8, 512), jnp.float32)], axis=0)

    pooled_mean = (all_sums / all_counts).astype(jnp.bfloat16)
    pre_norm = jnp.dot(pooled_mean, w_pool[...], preferred_element_type=jnp.float32) + b_pool[...]
    pooled_normed, pooled_inv = layer_stats(pre_norm)
    slope_grad = all_cot * gelu_slope(pooled_normed * pool_gain[...])
    grad_pre = norm_back(slope_grad * pool_gain[...], pooled_normed, pooled_inv)
    grad_pre_b = grad_pre.astype(jnp.bfloat16)
    share = against_rows(grad_pre_b, w_pool[...]) / all_counts
    share_b = share.astype(jnp.bfloat16)
    rest_b = (share - share_b.astype(jnp.float32)).astype(jnp.bfloat16)
    dmixed_main = inner_rows(member, share_b)
    dmixed_ref[...] = dmixed_main + inner_rows(member, rest_b)
    dmixed_b = dmixed_main.astype(jnp.bfloat16)
    datt = against_rows(dmixed_b, w_out[...]).astype(jnp.bfloat16)
    datt_f = datt.astype(jnp.float32)
    datt_ref[...] = (datt_f * 0.25).astype(jnp.bfloat16)
    product = datt_f * att[...].astype(jnp.float32)
    datt_t = against_rows(w_out[...], dmixed_b).astype(jnp.bfloat16).astype(jnp.float32)
    datt_t_ref[...] = (datt_t * 0.25).astype(jnp.bfloat16)
    slot = lax.broadcasted_iota(jnp.int32, (256, 256), 0)
    channel = lax.broadcasted_iota(jnp.int32, (256, 256), 1)
    spot = slot % HALF - LOG_LANE
    place = (channel // HALF == slot // HALF) & (spot >= 0) & (spot < 24)
    place = (place & (spot % PER_HALF == channel % HALF // HEAD_SIZE)).astype(jnp.float32)
    place = place.astype(jnp.bfloat16)
    first = product.astype(jnp.bfloat16)
    second = product - first.astype(jnp.float32)
    second_b = second.astype(jnp.bfloat16)
    third_b = (second - second_b.astype(jnp.float32)).astype(jnp.bfloat16)
    deltas = against_rows(place, first) + against_rows(place, second_b) + against_rows(place, third_b)
    which = (lax.broadcasted_iota(jnp.int32, (256, 1), 0) % HALF - LOG_LANE) // PER_HALF
    delta_ref[...] = split_three(deltas * -0.25, which).astype(jnp.bfloat16)
    gw_pool[...] = (inner_rows(pooled_mean[:HALF], grad_pre_b[:HALF]) * scale).astype(jnp.bfloat16)
    gw_out[...] = (inner_rows(att[...], dmixed_b) * scale).astype(jnp.bfloat16)
    gb_pool[...] = jnp.sum(grad_pre[:HALF], axis=0, keepdims=True) * scale
    g_gain[...] = jnp.sum(slope_grad[:HALF] * pooled_normed[:HALF], axis=0, keepdims=True) * scale


def pool(scale, *arrays):
    half = jnp.bfloat16
    vmem = pl.BlockSpec(memory_space=pltpu.VMEM)
    return pl.pallas_call(
        functools.partial(pool_kernel, scale),
        out_shape=[
            jax.ShapeDtypeStruct((PATCH, 256), jnp.float32),
            jax.ShapeDtypeStruct((PATCH, 256), half),
            jax.ShapeDtypeStruct((256, PATCH), half),
            jax.ShapeDtypeStruct((256, PATCH), half),
            jax.ShapeDtypeStruct((256, 512), half),
            jax.ShapeDtypeStruct((256, 256), half),
            jax.ShapeDtypeStruct((1, 512), jnp.float32),
            jax.ShapeDtypeStruct((1, 512), jnp.float32),
        ],
        in_specs=[vmem] * 9,
        out_specs=[vmem] * 8,
        scratch_shapes=[
            pltpu.VMEM((8, 384), jnp.float32),
            pltpu.VMEM((8, 896), jnp.float32),
            pltpu.VMEM((8, 384), jnp.float32),
            pltpu.VMEM((8, 896), jnp.float32),
            pltpu.SemaphoreType.DMA((2, 2)),
        ],
        compiler_params=pltpu.CompilerParams(
            collective_id=2, has_side_effects=True, vmem_limit_bytes=32 * 1024 * 1024
        ),
        name="pooling",
    )(*arrays)


def backward_kernel(
    spans, q_ref, qt_ref, logs_ref, do_ref, dot_ref, deltas_ref, kg_ref, vg_ref,
    dq_ref, dk_ref, dv_ref, qt, dt, qn, dn, some, slopes, dqt, dk_sum, dv_sum,
):
    tile = pl.program_id(1)
    start, count = spans[tile, 0], spans[tile, 1]
    q_both = jnp.concatenate([qt_ref[...], logs_ref[...]], axis=0)
    d_both = jnp.concatenate([dot_ref[...], deltas_ref[...]], axis=0)
    for h in range(PER_HALF):
        p, place = h // PAIR, slice(h % PAIR * TILE, (h % PAIR + 1) * TILE)
        rows = head_mask(h, 0)
        qt[p, :, place] = q_both * rows
        dt[p, :, place] = d_both * rows
        lanes = head_mask(h, 1)[:, :HALF]
        qn[p, place, :] = q_ref[...] * lanes
        dn[p, place, :] = do_ref[...] * lanes
    dqt[...] = jnp.zeros_like(dqt)

    @pl.when(tile == 0)
    def _():
        dk_sum[...] = jnp.zeros_like(dk_sum)
        dv_sum[...] = jnp.zeros_like(dv_sum)

    def chunk(c, carry):
        rows = pl.ds(pl.multiple_of(start + c * CHUNK, 16), CHUNK)
        keys_t = kg_ref[rows, :HALF].astype(jnp.float32).T.astype(jnp.bfloat16)
        for p in range(PER_HALF // PAIR):
            weights = jnp.exp(jnp.dot(kg_ref[rows, :], qt[p], preferred_element_type=jnp.float32))
            dweights = jnp.dot(vg_ref[rows, :], dt[p], preferred_element_type=jnp.float32)
            place = slice(p * PAIR * TILE, (p + 1) * PAIR * TILE)
            some[:, place] = weights.astype(jnp.bfloat16)
            slopes[:, place] = (weights * dweights).astype(jnp.bfloat16)
        depth = PER_HALF * TILE
        dk = jnp.dot(slopes[...], qn[...].reshape(depth, HALF), preferred_element_type=jnp.float32)
        dv = jnp.dot(some[...], dn[...].reshape(depth, HALF), preferred_element_type=jnp.float32)
        for p in range(PER_HALF // PAIR):
            own = slice(p * PAIR * HEAD_SIZE, (p + 1) * PAIR * HEAD_SIZE)
            place = slice(p * PAIR * TILE, (p + 1) * PAIR * TILE)
            dqt[own, :] += jnp.dot(keys_t[own], slopes[:, place], preferred_element_type=jnp.float32)
        dk_sum[rows, :] += dk
        dv_sum[rows, :] += dv
        return carry

    lax.fori_loop(0, count, chunk, 0)
    parts = []
    for h in range(PER_HALF):
        place = slice(h % PAIR * TILE, (h % PAIR + 1) * TILE)
        parts.append(dqt[h * HEAD_SIZE : (h + 1) * HEAD_SIZE, place])
    dq_ref[...] = jnp.concatenate(parts, axis=0).T.astype(jnp.bfloat16)

    @pl.when(tile == TILES - 1)
    def _():
        dk_ref[...] = (dk_sum[:WINDOW] * 4.0).astype(jnp.bfloat16)
        dv_ref[...] = (dv_sum[:WINDOW] * 4.0).astype(jnp.bfloat16)


def attend_back(spans, queries, queries_t, logs, douts, douts_t, deltas, keys_g, values_g):
    tall = pl.BlockSpec((None, TALL, 2 * HALF), lambda g, t: (g, 0, 0))
    mine = pl.BlockSpec((TILE, HALF), lambda g, t: (t, g))
    turned = pl.BlockSpec((HALF, TILE), lambda g, t: (g, t))
    sums = pl.BlockSpec((WINDOW, HALF), lambda g, t: (0, g))
    half = jnp.bfloat16
    return pl.pallas_call(
        backward_kernel,
        grid=(2, TILES),
        out_shape=[
            jax.ShapeDtypeStruct((PATCH, 256), half),
            jax.ShapeDtypeStruct((WINDOW, 256), half),
            jax.ShapeDtypeStruct((WINDOW, 256), half),
        ],
        in_specs=[pl.BlockSpec(memory_space=pltpu.SMEM)]
        + [mine, turned, turned, mine, turned, turned, tall, tall],
        out_specs=[mine, sums, sums],
        scratch_shapes=[
            pltpu.VMEM((PER_HALF // PAIR, 2 * HALF, PAIR * TILE), half),
            pltpu.VMEM((PER_HALF // PAIR, 2 * HALF, PAIR * TILE), half),
            pltpu.VMEM((PER_HALF // PAIR, PAIR * TILE, HALF), half),
            pltpu.VMEM((PER_HALF // PAIR, PAIR * TILE, HALF), half),
            pltpu.VMEM((CHUNK, 256 * PER_HALF // PAIR), half),
            pltpu.VMEM((CHUNK, 256 * PER_HALF // PAIR), half),
            pltpu.VMEM((HALF, PAIR * TILE), jnp.float32),
            pltpu.VMEM((TALL, HALF), jnp.float32),
            pltpu.VMEM((TALL, HALF), jnp.float32),
        ],
        compiler_params=pltpu.CompilerParams(vmem_limit_bytes=40 * 1024 * 1024),
        name="attention_back",
    )(spans, queries, queries_t, logs, douts, douts_t, deltas, keys_g, values_g)


UNIT = 128
EXTRA = 16
CORE_ROWS = 12 * UNIT
X_ROWS = CORE_ROWS // 4
Y_ROWS = X_ROWS // 8


def axes():
    me = lax.axis_index("pts")
    core, z, y, x = me % 2, (me // 2) % 8, (me // 16) % 8, me // 128
    return (
        (core, 2, lambda r: x * 128 + y * 16 + z * 2 + r),
        (x, 4, lambda r: r * 128 + y * 16 + z * 2 + core),
        (y, 8, lambda r: x * 128 + r * 16 + z * 2 + core),
        (z, 8, lambda r: x * 128 + y * 16 + r * 2 + core),
    )


def swap(axis, source, landing, sems, first):
    rank, size, device = axis
    copies = []
    for k in range(1, size):
        peer = (rank + k) % size
        copies.append(send(source(peer), landing(rank), sems, first + k - 1, device(peer)))
    return copies


def wait_all(copies):
    for copy in copies:
        copy.wait()


def slot_sum(ref, start, size):
    total = ref[0, start : start + size, :].astype(jnp.float32)
    for r in range(1, ref.shape[0]):
        total = total + ref[r, start : start + size, :].astype(jnp.float32)
    return total


def finish_kernel(
    scale, hidden, dq, dk, dv, dmixed, points, gain, w_qkv, gw_out, gw_pool, gb_pool, g_gain,
    grad_points, reduced, extras,
    low_k, low_v, high_k, high_v, send_c, recv_c, send_x, recv_x, send_y, recv_y, recv_z,
    gather_y, gather_x, gather_c, sems,
):
    me, before, after = neighbours()
    on_core, on_x, on_y, on_z = axes()
    barrier = pltpu.get_barrier_semaphore()
    greeted = [before, after]
    for rank, size, device in (on_core, on_x, on_y, on_z):
        greeted += [device((rank + k) % size) for k in range(1, size)]
    for device in greeted:
        pl.semaphore_signal(barrier, inc=1, device_id=(device,), device_id_type=MESH)

    def fill(block, first_unit):
        for column in range(block.shape[1] // UNIT):
            unit = first_unit + 2 * column
            start = unit % 12 * UNIT
            send_c[unit // 12, start : start + 2 * UNIT, :] = block[:, column * UNIT : (column + 1) * UNIT]

    fill(gw_out[...], 12)
    fill(gw_pool[...], 16)
    pieces = [gb_pool[:, i * UNIT : (i + 1) * UNIT] for i in range(4)]
    pieces += [g_gain[:, i * UNIT : (i + 1) * UNIT] for i in range(4)]
    pieces += [jnp.zeros((EXTRA - 8, UNIT), jnp.float32)]
    packed = jnp.concatenate(pieces, axis=0).astype(jnp.bfloat16)
    for r in range(2):
        send_c[r, CORE_ROWS:, :] = packed
    pl.semaphore_wait(barrier, len(greeted))
    rims = [
        send(dk.at[pl.ds(0, PATCH)], high_k, sems, 40, before),
        send(dv.at[pl.ds(0, PATCH)], high_v, sems, 41, before),
        send(dk.at[pl.ds(2 * PATCH, PATCH)], low_k, sems, 42, after),
        send(dv.at[pl.ds(2 * PATCH, PATCH)], low_v, sems, 43, after),
    ]
    own = slice(PATCH, 2 * PATCH)
    fill((inner_rows(hidden[own, :], dq[...]) * scale).astype(jnp.bfloat16), 0)
    fill((inner_rows(hidden[...], dk[...]) * scale).astype(jnp.bfloat16), 4)
    fill((inner_rows(hidden[...], dv[...]) * scale).astype(jnp.bfloat16), 8)

    copies = swap(on_core, lambda r: send_c.at[r], lambda r: recv_c, sems, 0)
    dhidden = against_rows(dq[...], w_qkv[:, :256])
    wait_all(copies)
    kept = send_c.at[on_core[0]]
    extra = (
        kept[CORE_ROWS:, :].astype(jnp.float32) + recv_c[CORE_ROWS:, :].astype(jnp.float32)
    ).astype(jnp.bfloat16)
    for r in range(4):
        rows = slice(r * X_ROWS, (r + 1) * X_ROWS)
        total = kept[rows, :].astype(jnp.float32) + recv_c[rows, :].astype(jnp.float32)
        send_x[r, :X_ROWS, :] = total.astype(jnp.bfloat16)
        send_x[r, X_ROWS:, :] = extra

    copies = swap(on_x, lambda r: send_x.at[r], lambda r: recv_x.at[r], sems, 1)
    recv_x[on_x[0]] = send_x[on_x[0]]
    wait_all(rims)
    for columns, mine, low, high in (
        (slice(256, 512), dk, low_k, high_k), (slice(512, 768), dv, low_v, high_v)
    ):
        total = mine[own, :].astype(jnp.float32) + low[...].astype(jnp.float32)
        total = (total + high[...].astype(jnp.float32)).astype(jnp.bfloat16)
        dhidden = dhidden + against_rows(total, w_qkv[:, columns])
    normed, inv_std = layer_stats(points[...].astype(jnp.float32))
    grad_points[...] = dmixed[...] + norm_back(dhidden * gain[...], normed, inv_std)
    wait_all(copies)
    extra = slot_sum(recv_x, X_ROWS, EXTRA).astype(jnp.bfloat16)
    for r in range(8):
        send_y[r, :Y_ROWS, :] = slot_sum(recv_x, r * Y_ROWS, Y_ROWS).astype(jnp.bfloat16)
        send_y[r, Y_ROWS:, :] = extra

    copies = swap(on_y, lambda r: send_y.at[r], lambda r: recv_y.at[r], sems, 4)
    recv_y[on_y[0]] = send_y[on_y[0]]
    wait_all(copies)
    recv_z[on_z[0]] = slot_sum(recv_y, 0, Y_ROWS + EXTRA).astype(jnp.bfloat16)

    wait_all(swap(on_z, lambda r: recv_z.at[on_z[0]], lambda r: recv_z.at[r], sems, 11))
    total = slot_sum(recv_z, 0, Y_ROWS + EXTRA)
    extras[...] = total[Y_ROWS:]
    gather_y[on_y[0]] = total[:Y_ROWS].astype(jnp.bfloat16)
    wait_all(swap(on_y, lambda r: gather_y.at[on_y[0]], lambda r: gather_y.at[r], sems, 18))
    gather_x[on_x[0]] = gather_y[...]
    copies = swap(on_x, lambda r: gather_y, lambda r: gather_x.at[r], sems, 25)
    wait_all(copies)
    gather_c[on_core[0]] = gather_x[...]
    wait_all(swap(on_core, lambda r: gather_x, lambda r: gather_c.at[r], sems, 28))
    for c in range(2):
        for r in range(4):
            for s in range(8):
                start = c * CORE_ROWS + r * X_ROWS + s * Y_ROWS
                reduced[start : start + Y_ROWS, :] = gather_c[c, r, s]
    weighted = jnp.zeros((256, UNIT), jnp.float32)
    for column in range(6):
        block = reduced[column * 256 : (column + 1) * 256, :].astype(jnp.float32)
        lanes = slice(column * UNIT, (column + 1) * UNIT)
        weighted = weighted + block * w_qkv[:, lanes].astype(jnp.float32)
    summed_gain = jnp.sum(weighted.T, axis=0, keepdims=True) / gain[...]
    for i in range(2):
        extras[8 + i : 9 + i, :] = summed_gain[:, i * UNIT : (i + 1) * UNIT]


def finish(scale, *arrays):
    half = jnp.bfloat16
    vmem = pl.BlockSpec(memory_space=pltpu.VMEM)
    return pl.pallas_call(
        functools.partial(finish_kernel, scale),
        out_shape=[
            jax.ShapeDtypeStruct((PATCH, 256), jnp.float32),
            jax.ShapeDtypeStruct((2 * CORE_ROWS, UNIT), half),
            jax.ShapeDtypeStruct((EXTRA, UNIT), jnp.float32),
        ],
        in_specs=[vmem] * 12,
        out_specs=[vmem] * 3,
        scratch_shapes=[pltpu.VMEM((PATCH, 256), half)] * 4
        + [
            pltpu.VMEM((2, CORE_ROWS + EXTRA, UNIT), half),
            pltpu.VMEM((CORE_ROWS + EXTRA, UNIT), half),
            pltpu.VMEM((4, X_ROWS + EXTRA, UNIT), half),
            pltpu.VMEM((4, X_ROWS + EXTRA, UNIT), half),
            pltpu.VMEM((8, Y_ROWS + EXTRA, UNIT), half),
            pltpu.VMEM((8, Y_ROWS + EXTRA, UNIT), half),
            pltpu.VMEM((8, Y_ROWS + EXTRA, UNIT), half),
            pltpu.VMEM((8, Y_ROWS, UNIT), half),
            pltpu.VMEM((4, 8, Y_ROWS, UNIT), half),
            pltpu.VMEM((2, 4, 8, Y_ROWS, UNIT), half),
            pltpu.SemaphoreType.DMA((2, 44)),
        ],
        compiler_params=pltpu.CompilerParams(
            collective_id=3, has_side_effects=True, vmem_limit_bytes=40 * 1024 * 1024
        ),
        name="finish",
    )(*arrays)


def unpack_kernel(reduced, extras, rows_in, gq, go, gn, gp, gb, gg, rows_out, sem):
    copy = pltpu.make_async_copy(rows_in, rows_out, sem)
    copy.start()
    for column in range(12):
        block = reduced[column * 256 : (column + 1) * 256, :].astype(jnp.float32)
        if column < 6:
            gq[:, column * UNIT : (column + 1) * UNIT] = block
        elif column < 8:
            go[:, (column - 6) * UNIT : (column - 5) * UNIT] = block
        else:
            gp[:, (column - 8) * UNIT : (column - 7) * UNIT] = block
    for i in range(2):
        gn[:, i * UNIT : (i + 1) * UNIT] = extras[8 + i : 9 + i, :]
    for i in range(4):
        gb[:, i * UNIT : (i + 1) * UNIT] = extras[i : i + 1, :]
        gg[:, i * UNIT : (i + 1) * UNIT] = extras[4 + i : 5 + i, :]
    copy.wait()


def unpack(reduced, extras, rows):
    vmem = pl.BlockSpec(memory_space=pltpu.VMEM)
    outside = pl.BlockSpec(memory_space=pl.ANY)
    shapes = ((256, 768), (256, 256), (1, 256), (256, 512), (1, 512), (1, 512), (PATCH, 256))
    return pl.pallas_call(
        unpack_kernel,
        out_shape=[jax.ShapeDtypeStruct(shape, jnp.float32) for shape in shapes],
        in_specs=[vmem, vmem, vmem],
        out_specs=[vmem] * 6 + [outside],
        scratch_shapes=[pltpu.SemaphoreType.DMA],
        name="unpack",
    )(reduced, extras, rows)


def body(
    points, patch_ids, cell_ids, norm_gain, w_qkv, w_out, w_pool, b_pool, pool_gain, cotangent
):
    scale = 1.0 / math.sqrt(points.shape[0] * lax.axis_size("pts"))
    gain = norm_gain[None]
    cells = cell_ids.reshape(4, HALF)
    queries, queries_t, keys_g, values_g, marks_f, hidden, spans = prepare(
        points, patch_ids.reshape(4, HALF), gain, w_qkv
    )
    attended, logs, sums, counts = attend(
        spans, queries_t, marks_f, keys_g, values_g, points, w_out, cells
    )
    dmixed, datt, datt_t, deltas, gw_pool, gw_out, gb_pool, g_gain = pool(
        scale, sums, counts, cells, attended, w_out, w_pool, b_pool[None], pool_gain[None], cotangent
    )
    dq, dk, dv = attend_back(
        spans, queries, queries_t, logs, datt, datt_t, deltas, keys_g, values_g
    )
    grad_points, reduced, extras = finish(
        scale, hidden, dq, dk, dv, dmixed, points, gain, w_qkv, gw_out, gw_pool, gb_pool, g_gain
    )
    gq, go, gn, gp, gb, gg, grad_points = unpack(reduced, extras, grad_points)
    return (grad_points, gq, go, gn[0], gp, gb[0], gg[0])


def solution(mesh):
    in_specs = (P("pts", None), P("pts"), P("pts"), P(), P(), P(), P(), P(), P(), P("pts", None))
    out_specs = (P("pts", None), P(), P(), P(), P(), P(), P())
    return jax.shard_map(body, mesh=mesh, in_specs=in_specs, out_specs=out_specs, check_vma=False)
```

profile of v0, /device:TPU:1, one launch (start us, length us, event | category | flops | bytes accessed | tf_op | source)
XLA Modules:
  0.0 119.0 jit_solution(1369845040344217917)
XLA Ops:
  0.6 0.0 copy-start
  0.6 0.9 copy-done
  1.6 0.0 copy-start.3
  1.6 1.0 copy-done.3
  2.6 0.0 copy-start.12
  2.6 0.7 copy-done.12
  3.3 0.0 copy-start.14
  3.3 0.7 copy-done.14
  3.9 19.0 %prepare.1 = (bf16[512,256]{1,0:T(8,128)(2,1)S(1)}, bf16[256,512]{1,0:T(8,128)(2,1)S(1)}, bf16[2,1584,256]{2,1,0:T(8,128)(2,1)S(1)}, bf16[2,1584,256]{2,1,0:T(8,...) custom-call(bf16[512,256]{1,0:T(8,128)(2,1)S(1)} %copy-done, ...), custom_call_target="tpu_custom_call" | custom-call | tf_op jit(solution)/shard_map/prepare/pallas_call | solution.py:203
  23.0 0.0 copy-start.1
  23.0 0.9 copy-done.1
  23.9 0.0 copy-start.6
  23.9 0.9 copy-done.6
  24.8 0.0 copy-start.11
  24.8 0.7 copy-done.11
  25.5 0.0 copy-start.8
  25.5 0.0 copy-start.9
  25.5 0.0 copy-start.15
  25.5 0.0 copy-start.16
  25.5 13.0 %attention.1 = (bf16[512,256]{1,0:T(8,128)(2,1)S(1)}, bf16[256,512]{1,0:T(8,128)(2,1)S(1)}, f32[144,256]{1,0:T(8,128)S(1)}, f32[144,128]{1,0:T(8,128)S(1)}) custom-call(s32[4,2]{1,0:T(4,128)S(1)} %get-tuple-element.40.spans, bf16[256,512]{1,0:T(8,128)(2,1)S(1)} %get-tuple-element.42.qt_ref, bf16[128,512]{1,0:T(8,128)(2,1)S(1)} %get-tuple-element.43.f_ref, ...), custom_call_target="tpu_custom_call" | custom-call | tf_op jit(solution)/shard_map/attention/pallas_call | solution.py:343
  38.5 0.0 copy-done.8
  38.5 0.0 copy-done.9
  38.5 0.0 copy-done.15
  38.5 0.0 copy-done.16
  38.5 13.4 %pooling.1 = (f32[512,256]{1,0:T(8,128)S(1)}, bf16[512,256]{1,0:T(8,128)(2,1)S(1)}, bf16[256,512]{1,0:T(8,128)(2,1)S(1)}, bf16[256,512]{1,0:T(8,128)(2,1)S(1)}, ...) custom-call(f32[144,256]{1,0:T(8,128)S(1)} %get-tuple-element.47.sums,, ...), custom_call_target="tpu_custom_call" | custom-call | tf_op jit(solution)/shard_map/pooling/pallas_call | solution.py:458
  52.0 0.0 copy-start.2
  52.0 0.0 copy-start.4
  52.0 0.0 copy-start.13
  52.0 19.2 %attention_back.1 = (bf16[512,256]{1,0:T(8,128)(2,1)S(1)}, bf16[1536,256]{1,0:T(8,128)(2,1)S(1)}, bf16[1536,256]{1,0:T(8,128)(2,1)S(1)}) custom-call(s32[4,2]{1,0:T(4,128)S(1)} %get-tuple-element.40.spans, bf16[512,256]{1,0:T(8,128)(2,1)S(1)} %get-tuple-element.41.q_ref, bf16[256,512]{1,0:T(8,128)(2,1)S(1)} %get-tuple-element.42.qt_ref, ...), custom_call_target="tpu_custom_call" | custom-call | tf_op jit(solution)/shard_map/attention_back/pallas_call | solution.py:548
  71.2 0.0 copy-done.2
  71.2 0.0 copy-done.4
  71.2 0.0 copy-done.13
  71.2 42.3 %finish.1 = (f32[512,256]{1,0:T(8,128)S(1)}, bf16[3072,128]{1,0:T(8,128)(2,1)S(1)}, f32[16,128]{1,0:T(8,128)S(1)}) custom-call(bf16[1536,256]{1,0:T(8,128)(2,1)S(1)} %get-tuple-element.39.hidden, bf16[512,256]{1,0:T(8,128)(2,1)S(1)} %get-tuple-element.53.dq, bf16[1536,256]{1,0:T(8,128)(2,1)S(1)} %get-tuple-element.54.dk, ...), custom_call_target="tpu_custom_call" | custom-call | tf_op jit(solution)/shard_map/finish/pallas_call | solution.py:718
  113.5 0.0 copy-start.5
  113.5 0.9 copy-done.5
  114.4 0.0 copy-start.7
  114.4 0.8 copy-done.7
  115.2 0.0 copy-start.10
  115.2 0.6 copy-done.10
  115.8 3.2 %unpack.1 = (f32[256,768]{1,0:T(8,128)}, f32[256,256]{1,0:T(8,128)}, f32[1,256]{1,0:T(1,128)}, f32[256,512]{1,0:T(8,128)}, f32[1,512]{1,0:T(1,128)}, /*index=5*/f32[1,512]{1,0:T(1,128)}, f32[512,256]{1,0:T(8,128)}) custom-call(bf16[3072,128]{1,0:T(8,128)(2,1)} %copy-done.5, f32[16,128]{1,0:T(8,128)} %copy-done.10, f32[512,256]{1,0:T(8,128)} %copy-done.7), custom_call_target="tpu_custom_call" | custom-call | tf_op jit(solution)/shard_map/unpack/pallas_call | solution.py:771
Async XLA Ops:
  0.6 1.0 copy-start
  1.6 1.0 copy-start.3
  2.6 0.7 copy-start.12
  3.3 0.7 copy-start.14
  23.0 1.0 copy-start.1
  23.9 0.9 copy-start.6
  24.8 0.7 copy-start.11
  25.5 13.0 %copy-start.8 = (bf16[256,512]{1,0:T(8,128)(2,1)S(1)}, bf16[256,512]{1,0:T(8,128)(2,1)}, u32[]{:S(2)}) copy-start(bf16[256,512]{1,0:T(8,128)(2,1)} %w_pool.1) | copy-start | bytes 786436
  25.5 13.0 %copy-start.9 = (f32[128,512]{1,0:T(8,128)S(1)}, f32[128,512]{1,0:T(8,128)}, u32[]{:S(2)}) copy-start(f32[128,512]{1,0:T(8,128)} %cotangent.1) | copy-start | bytes 786436
  25.5 13.0 %copy-start.15 = (f32[512]{0:T(512)S(1)}, f32[512]{0:T(512)}, u32[]{:S(2)}) copy-start(f32[512]{0:T(512)} %param.17) | copy-start | bytes 6148
  25.5 13.0 %copy-start.16 = (f32[512]{0:T(512)S(1)}, f32[512]{0:T(512)}, u32[]{:S(2)}) copy-start(f32[512]{0:T(512)} %param.18) | copy-start | bytes 6148
  52.0 19.2 %copy-start.2 = (bf16[512,256]{1,0:T(8,128)(2,1)S(1)}, bf16[512,256]{1,0:T(8,128)(2,1)}, u32[]{:S(2)}) copy-start(bf16[512,256]{1,0:T(8,128)(2,1)} %points.1) | copy-start | bytes 786436
  52.0 19.2 %copy-start.4 = (bf16[256,768]{1,0:T(8,128)(2,1)S(1)}, bf16[256,768]{1,0:T(8,128)(2,1)}, u32[]{:S(2)}) copy-start(bf16[256,768]{1,0:T(8,128)(2,1)} %w_qkv.1) | copy-start | bytes 1179652
  52.0 19.2 %copy-start.13 = (f32[256]{0:T(256)S(1)}, f32[256]{0:T(256)}, u32[]{:S(2)}) copy-start(f32[256]{0:T(256)} %param.13) | copy-start | bytes 3076
  113.5 0.9 copy-start.5
  114.4 0.8 copy-start.7
  115.2 0.6 copy-start.10
where the time goes:
time: 119 us
  Pallas kernels  110 us (92%)
  local copies, waits for them, and re-layouts  8.14 us (7%)
    pallas_call x1, Pallas kernels, finish(): pl.pallas_call(functools.partial(finish_kernel, scale), out_shape=[jax.Sh...  42.3 us
    pallas_call x1, Pallas kernels, attend_back(): pl.pallas_call(backward_kernel, grid=(2, TILES), out_shape=[jax.ShapeDtyp...  19.2 us
    pallas_call x1, Pallas kernels, prepare(): pl.pallas_call(prepare_kernel, out_shape=[jax.ShapeDtypeStruct((PATCH, 25...  19 us
    pallas_call x1, Pallas kernels, pool(): pl.pallas_call(functools.partial(pool_kernel, scale), out_shape=[jax.Shap...  13.4 us
    pallas_call x1, Pallas kernels, attend(): pl.pallas_call(forward_kernel, grid=(TILES, 2), out_shape=[jax.ShapeDtype...  13 us
    unnamed x34, local copies, waits for them, and re-layouts  8.14 us
    pallas_call x1, Pallas kernels, unpack(): pl.pallas_call(unpack_kernel, out_shape=[jax.ShapeDtypeStruct(shape, jnp....  3.24 us

commit v1 on v0

--- a/solution.py
+++ b/solution.py
@@ -211,7 +211,7 @@
             jax.ShapeDtypeStruct((WINDOW, 256), half),
             jax.ShapeDtypeStruct((TILES, 2), jnp.int32),
         ],
-        in_specs=[pl.BlockSpec(memory_space=pl.ANY)] * 4,
+        in_specs=[pl.BlockSpec(memory_space=pltpu.HBM)] * 4,
         out_specs=[vmem] * 6 + [pl.BlockSpec(memory_space=pltpu.SMEM)],
         scratch_shapes=[
             pltpu.VMEM((PATCH, 256), half),
@@ -339,7 +339,7 @@
     def whole(*shape):
         return pl.BlockSpec(shape, lambda t, g: (0,) * len(shape))
 
-    outside = pl.BlockSpec(memory_space=pl.ANY)
+    outside = pl.BlockSpec(memory_space=pltpu.HBM)
     return pl.pallas_call(
         forward_kernel,
         grid=(TILES, 2),
@@ -640,19 +640,19 @@
     packed = jnp.concatenate(pieces, axis=0).astype(jnp.bfloat16)
     for r in range(2):
         send_c[r, CORE_ROWS:, :] = packed
+    own = slice(PATCH, 2 * PATCH)
+    fill((inner_rows(hidden[own, :], dq[...]) * scale).astype(jnp.bfloat16), 0)
+    fill((inner_rows(hidden[...], dk[...]) * scale).astype(jnp.bfloat16), 4)
+    fill((inner_rows(hidden[...], dv[...]) * scale).astype(jnp.bfloat16), 8)
+
     pl.semaphore_wait(barrier, len(greeted))
+    copies = swap(on_core, lambda r: send_c.at[r], lambda r: recv_c, sems, 0)
     rims = [
         send(dk.at[pl.ds(0, PATCH)], high_k, sems, 40, before),
         send(dv.at[pl.ds(0, PATCH)], high_v, sems, 41, before),
         send(dk.at[pl.ds(2 * PATCH, PATCH)], low_k, sems, 42, after),
         send(dv.at[pl.ds(2 * PATCH, PATCH)], low_v, sems, 43, after),
     ]
-    own = slice(PATCH, 2 * PATCH)
-    fill((inner_rows(hidden[own, :], dq[...]) * scale).astype(jnp.bfloat16), 0)
-    fill((inner_rows(hidden[...], dk[...]) * scale).astype(jnp.bfloat16), 4)
-    fill((inner_rows(hidden[...], dv[...]) * scale).astype(jnp.bfloat16), 8)
-
-    copies = swap(on_core, lambda r: send_c.at[r], lambda r: recv_c, sems, 0)
     dhidden = against_rows(dq[...], w_qkv[:, :256])
     wait_all(copies)
     kept = send_c.at[on_core[0]]
@@ -774,6 +774,7 @@
         in_specs=[vmem, vmem, vmem],
         out_specs=[vmem] * 6 + [outside],
         scratch_shapes=[pltpu.SemaphoreType.DMA],
+        compiler_params=pltpu.CompilerParams(vmem_limit_bytes=16 * 1024 * 1024),
         name="unpack",
     )(reduced, extras, rows)
 
@@ -784,11 +785,13 @@
     scale = 1.0 / math.sqrt(points.shape[0] * lax.axis_size("pts"))
     gain = norm_gain[None]
     cells = cell_ids.reshape(4, HALF)
-    queries, queries_t, keys_g, values_g, marks_f, hidden, spans = prepare(
-        points, patch_ids.reshape(4, HALF), gain, w_qkv
-    )
+    far = [
+        pltpu.with_memory_space_constraint(array, pltpu.HBM)
+        for array in (points, patch_ids.reshape(4, HALF), gain, w_qkv, w_out, cells)
+    ]
+    queries, queries_t, keys_g, values_g, marks_f, hidden, spans = prepare(*far[:4])
     attended, logs, sums, counts = attend(
-        spans, queries_t, marks_f, keys_g, values_g, points, w_out, cells
+        spans, queries_t, marks_f, keys_g, values_g, far[0], far[4], far[5]
     )
     dmixed, datt, datt_t, deltas, gw_pool, gw_out, gb_pool, g_gain = pool(
         scale, sums, counts, cells, attended, w_out, w_pool, b_pool[None], pool_gain[None], cotangent

time: 119 us -> 111 us (0.933)
  local copies, waits for them, and re-layouts: 8.14 us -> 0.06 us
    unnamed x34 -> x18, local copies, waits for them, and re-layouts: 8.14 us -> 0.06 us
    pallas_call x1, Pallas kernels: 3.24 us -> 1.95 us  [unpack(): pl.pallas_call(unpack_kernel, out_shape=[jax.ShapeDtypeStruct(shape, jnp....]
where the time goes in v1:
time: 111 us; the launch traced here: 110 us
  Pallas kernels  109 us (98%)
    pallas_call x1, Pallas kernels, finish(): pl.pallas_call(functools.partial(finish_kernel, scale), out_shape=[jax.Sh...  43.4 us
    pallas_call x1, Pallas kernels, attend_back(): pl.pallas_call(backward_kernel, grid=(2, TILES), out_shape=[jax.ShapeDtyp...  19.2 us
    pallas_call x1, Pallas kernels, prepare(): pl.pallas_call(prepare_kernel, out_shape=[jax.ShapeDtypeStruct((PATCH, 25...  18.8 us
    pallas_call x1, Pallas kernels, pool(): pl.pallas_call(functools.partial(pool_kernel, scale), out_shape=[jax.Shap...  13.4 us
    pallas_call x1, Pallas kernels, attend(): pl.pallas_call(forward_kernel, grid=(TILES, 2), out_shape=[jax.ShapeDtype...  12.7 us

profile of v1, /device:TPU:1, one launch (start us, length us, event | category | flops | bytes accessed | tf_op | source)
XLA Modules:
  0.0 110.3 jit_solution(14504088918939267505)
XLA Ops:
  0.6 18.8 %prepare.1 = (bf16[512,256]{1,0:T(8,128)(2,1)S(1)}, bf16[256,512]{1,0:T(8,128)(2,1)S(1)}, bf16[2,1584,256]{2,1,0:T(8,128)(2,1)S(1)}, bf16[2,1584,256]{2,1,0:T(8,...) custom-call(bf16[512,256]{1,0:T(8,128)(2,1)} %points.1, ...), custom_call_target="tpu_custom_call" | custom-call | tf_op jit(solution)/shard_map/prepare/pallas_call | solution.py:203
  19.5 0.0 copy-start.2
  19.5 0.0 copy-start.3
  19.5 0.0 copy-start.4
  19.5 0.0 copy-start.5
  19.5 0.0 copy-start.7
  19.5 0.0 copy-start.8
  19.5 12.7 %attention.1 = (bf16[512,256]{1,0:T(8,128)(2,1)S(1)}, bf16[256,512]{1,0:T(8,128)(2,1)S(1)}, f32[144,256]{1,0:T(8,128)S(1)}, f32[144,128]{1,0:T(8,128)S(1)}) custom-call(s32[4,2]{1,0:T(4,128)S(1)} %get-tuple-element.40.spans, bf16[256,512]{1,0:T(8,128)(2,1)S(1)} %get-tuple-element.42.qt_ref, bf16[128,512]{1,0:T(8,128)(2,1)S(1)} %get-tuple-element.43.f_ref, ...), custom_call_target="tpu_custom_call" | custom-call | tf_op jit(solution)/shard_map/attention/pallas_call | solution.py:343
  32.2 0.0 copy-done.2
  32.3 0.0 copy-done.3
  32.3 0.0 copy-done.4
  32.3 0.0 copy-done.5
  32.3 0.0 copy-done.7
  32.3 0.0 copy-done.8
  32.3 13.4 %pooling.1 = (f32[512,256]{1,0:T(8,128)S(1)}, bf16[512,256]{1,0:T(8,128)(2,1)S(1)}, bf16[256,512]{1,0:T(8,128)(2,1)S(1)}, bf16[256,512]{1,0:T(8,128)(2,1)S(1)}, ...) custom-call(f32[144,256]{1,0:T(8,128)S(1)} %get-tuple-element.47.sums,, ...), custom_call_target="tpu_custom_call" | custom-call | tf_op jit(solution)/shard_map/pooling/pallas_call | solution.py:458
  45.7 0.0 copy-start
  45.8 0.0 copy-start.1
  45.8 0.0 copy-start.6
  45.8 19.2 %attention_back.1 = (bf16[512,256]{1,0:T(8,128)(2,1)S(1)}, bf16[1536,256]{1,0:T(8,128)(2,1)S(1)}, bf16[1536,256]{1,0:T(8,128)(2,1)S(1)}) custom-call(s32[4,2]{1,0:T(4,128)S(1)} %get-tuple-element.40.spans, bf16[512,256]{1,0:T(8,128)(2,1)S(1)} %get-tuple-element.41.q_ref, bf16[256,512]{1,0:T(8,128)(2,1)S(1)} %get-tuple-element.42.qt_ref, ...), custom_call_target="tpu_custom_call" | custom-call | tf_op jit(solution)/shard_map/attention_back/pallas_call | solution.py:548
  64.9 0.0 copy-done
  64.9 0.0 copy-done.1
  65.0 0.0 copy-done.6
  65.0 43.4 %finish.1 = (f32[512,256]{1,0:T(8,128)S(1)}, bf16[3072,128]{1,0:T(8,128)(2,1)S(1)}, f32[16,128]{1,0:T(8,128)S(1)}) custom-call(bf16[1536,256]{1,0:T(8,128)(2,1)S(1)} %get-tuple-element.39.hidden, bf16[512,256]{1,0:T(8,128)(2,1)S(1)} %get-tuple-element.53.dq, bf16[1536,256]{1,0:T(8,128)(2,1)S(1)} %get-tuple-element.54.dk, ...), custom_call_target="tpu_custom_call" | custom-call | tf_op jit(solution)/shard_map/finish/pallas_call | solution.py:718
  108.4 1.9 %unpack.1 = (f32[256,768]{1,0:T(8,128)}, f32[256,256]{1,0:T(8,128)}, f32[1,256]{1,0:T(1,128)}, f32[256,512]{1,0:T(8,128)}, f32[1,512]{1,0:T(1,128)}, /*index=5*/f32[1,512]{1,0:T(1,128)}, f32[512,256]{1,0:T(8,128)}) custom-call(bf16[3072,128]{1,0:T(8,128)(2,1)S(1)} %get-tuple-element.61.reduced, f32[16,128]{1,0:T(8,128)S(1)} %get-tuple-element.62.extras, ...), custom_call_target="tpu_custom_call" | custom-call | tf_op jit(solution)/shard_map/unpack/pallas_call | solution.py:771
Async XLA Ops:
  19.5 12.8 %copy-start.2 = (bf16[256,256]{1,0:T(8,128)(2,1)S(1)}, bf16[256,256]{1,0:T(8,128)(2,1)}, u32[]{:S(2)}) copy-start(bf16[256,256]{1,0:T(8,128)(2,1)} %w_out.1) | copy-start | bytes 393220
  19.5 12.8 %copy-start.3 = (bf16[256,512]{1,0:T(8,128)(2,1)S(1)}, bf16[256,512]{1,0:T(8,128)(2,1)}, u32[]{:S(2)}) copy-start(bf16[256,512]{1,0:T(8,128)(2,1)} %w_pool.1) | copy-start | bytes 786436
  19.5 12.8 %copy-start.4 = (f32[128,512]{1,0:T(8,128)S(1)}, f32[128,512]{1,0:T(8,128)}, u32[]{:S(2)}) copy-start(f32[128,512]{1,0:T(8,128)} %cotangent.1) | copy-start | bytes 786436
  19.5 12.8 %copy-start.5 = (s32[512]{0:T(512)S(1)}, s32[512]{0:T(512)}, u32[]{:S(2)}) copy-start(s32[512]{0:T(512)} %param.12) | copy-start | bytes 6148
  19.5 12.8 %copy-start.7 = (f32[512]{0:T(512)S(1)}, f32[512]{0:T(512)}, u32[]{:S(2)}) copy-start(f32[512]{0:T(512)} %param.17) | copy-start | bytes 6148
  19.5 12.8 %copy-start.8 = (f32[512]{0:T(512)S(1)}, f32[512]{0:T(512)}, u32[]{:S(2)}) copy-start(f32[512]{0:T(512)} %param.18) | copy-start | bytes 6148
  45.7 19.2 %copy-start = (bf16[512,256]{1,0:T(8,128)(2,1)S(1)}, bf16[512,256]{1,0:T(8,128)(2,1)}, u32[]{:S(2)}) copy-start(bf16[512,256]{1,0:T(8,128)(2,1)} %points.1) | copy-start | bytes 786436
  45.8 19.2 %copy-start.1 = (bf16[256,768]{1,0:T(8,128)(2,1)S(1)}, bf16[256,768]{1,0:T(8,128)(2,1)}, u32[]{:S(2)}) copy-start(bf16[256,768]{1,0:T(8,128)(2,1)} %w_qkv.1) | copy-start | bytes 1179652
  45.8 19.2 %copy-start.6 = (f32[256]{0:T(256)S(1)}, f32[256]{0:T(256)}, u32[]{:S(2)}) copy-start(f32[256]{0:T(256)} %param.13) | copy-start | bytes 3076

commit v2 on v1

--- a/solution.py
+++ b/solution.py
@@ -252,27 +252,55 @@
     return jnp.max(folded, axis=0, keepdims=True)
 
 
+def block_of(index, size):
+    return pl.ds(pl.multiple_of(index * size, size), size)
+
+
 def forward_kernel(
     spans, qt_ref, f_ref, kg_ref, vg_ref, points_hbm, w_out_hbm, cells_hbm,
     att_ref, logs_ref, sums_ref, counts_ref, qt, kept, att_t, top_t, total_t, points, w_out, cells, sems,
 ):
-    tile, half = pl.program_id(0), pl.program_id(1)
-    start, count = spans[tile, 0], spans[tile, 1]
     late = [
         pltpu.make_async_copy(source, target, sems.at[i])
         for i, (source, target) in enumerate(
             ((points_hbm, points), (w_out_hbm, w_out), (cells_hbm, cells))
         )
     ]
-
-    @pl.when((tile == 0) & (half == 0))
-    def _():
-        for copy in late:
-            copy.start()
-
-    both = jnp.concatenate([qt_ref[...], f_ref[...]], axis=0)
+    for copy in late:
+        copy.start()
+    qt[...] = jnp.zeros_like(qt)
+
+    def step(index, carry):
+        forward_step(
+            index // 2, index % 2, spans, qt_ref, f_ref, kg_ref, vg_ref, att_ref, logs_ref,
+            qt, kept, att_t, top_t, total_t,
+        )
+        return carry
+
+    lax.fori_loop(0, 2 * TILES, step, 0)
+    for copy in late:
+        copy.wait()
+    mixed = points[...].astype(jnp.float32) + jnp.dot(
+        att_ref[...], w_out[...], preferred_element_type=jnp.float32
+    )
+    member = membership(cells[...])
+    sums_ref[...] = jnp.dot(
+        member.astype(jnp.bfloat16), mixed.astype(jnp.bfloat16), preferred_element_type=jnp.float32
+    )
+    counts_ref[...] = jnp.broadcast_to(jnp.sum(member, axis=1, keepdims=True), (SLOTS, HALF))
+
+
+def forward_step(
+    tile, half, spans, qt_ref, f_ref, kg_ref, vg_ref, att_ref, logs_ref, qt, kept, att_t, top_t, total_t
+):
+    start, count = spans[tile, 0], spans[tile, 1]
+    mine, turned = block_of(tile, TILE), block_of(half, HALF)
+    queries_t, marks = qt_ref[turned, mine], f_ref[:LOG_LANE, mine]
     for h in range(PER_HALF):
-        qt[h // PAIR, :, h % PAIR * TILE : (h % PAIR + 1) * TILE] = both * head_mask(h, 0)
+        place = slice(h % PAIR * TILE, (h % PAIR + 1) * TILE)
+        own = slice(h * HEAD_SIZE, (h + 1) * HEAD_SIZE)
+        qt[h // PAIR, own, place] = queries_t[own]
+        qt[h // PAIR, HALF : HALF + LOG_LANE, place] = marks
     top_t[...] = jnp.full_like(top_t, -3e38)
     total_t[...] = jnp.zeros_like(total_t)
     att_t[...] = jnp.zeros_like(att_t)
@@ -300,71 +328,35 @@
         return carry
 
     lax.fori_loop(0, count, chunk, 0)
-    rows = pl.ds(pl.multiple_of(tile * TILE, TILE), TILE)
     logs_p = -(top_t[...] + jnp.log(total_t[...]))
     parts, logs = [], []
     for h in range(PER_HALF):
         p, columns = h // PAIR, slice(h % PAIR * TILE, (h % PAIR + 1) * TILE)
-        mine = att_t[h * HEAD_SIZE : (h + 1) * HEAD_SIZE, columns]
-        parts.append(mine / total_t[p : p + 1, columns])
+        piece = att_t[h * HEAD_SIZE : (h + 1) * HEAD_SIZE, columns]
+        parts.append(piece / total_t[p : p + 1, columns])
         logs.append(logs_p[p : p + 1, columns])
     attended = jnp.concatenate(parts, axis=0).T.astype(jnp.bfloat16)
-    for g in range(2):
-
-        @pl.when(half == g)
-        def _():
-            att_ref[rows, g * HALF : (g + 1) * HALF] = attended
-
+    att_ref[mine, turned] = attended
     logs = jnp.concatenate(logs, axis=0)
     terms = [split_three(logs, i) for i in range(3)]
-    logs_ref[:LOG_LANE, :] = f_ref[:LOG_LANE, :]
     spare = jnp.zeros((HALF - LOG_LANE - 24, TILE), jnp.float32)
-    logs_ref[LOG_LANE:, :] = jnp.concatenate(terms + [spare], axis=0).astype(jnp.bfloat16)
-
-    @pl.when((tile == TILES - 1) & (half == 1))
-    def _():
-        for copy in late:
-            copy.wait()
-        mixed = points[...].astype(jnp.float32) + jnp.dot(
-            att_ref[...], w_out[...], preferred_element_type=jnp.float32
-        )
-        member = membership(cells[...])
-        sums_ref[...] = jnp.dot(
-            member.astype(jnp.bfloat16), mixed.astype(jnp.bfloat16), preferred_element_type=jnp.float32
-        )
-        counts_ref[...] = jnp.broadcast_to(jnp.sum(member, axis=1, keepdims=True), (SLOTS, HALF))
+    ending = jnp.concatenate(terms + [spare], axis=0).astype(jnp.bfloat16)
+    logs_ref[turned, mine] = jnp.concatenate([marks, ending], axis=0)
 
 
 def attend(spans, queries_t, marks_f, keys_g, values_g, points, w_out, cells):
-    def whole(*shape):
-        return pl.BlockSpec(shape, lambda t, g: (0,) * len(shape))
-
+    vmem = pl.BlockSpec(memory_space=pltpu.VMEM)
     outside = pl.BlockSpec(memory_space=pltpu.HBM)
     return pl.pallas_call(
         forward_kernel,
-        grid=(TILES, 2),
         out_shape=[
             jax.ShapeDtypeStruct((PATCH, 256), jnp.bfloat16),
             jax.ShapeDtypeStruct((256, PATCH), jnp.bfloat16),
             jax.ShapeDtypeStruct((SLOTS, 256), jnp.float32),
             jax.ShapeDtypeStruct((SLOTS, HALF), jnp.float32),
         ],
-        in_specs=[
-            pl.BlockSpec(memory_space=pltpu.SMEM),
-            pl.BlockSpec((HALF, TILE), lambda t, g: (g, t)),
-            pl.BlockSpec((HALF, TILE), lambda t, g: (0, t)),
-            whole(2, TALL, 2 * HALF),
-            whole(2, TALL, 2 * HALF),
-            outside,
-            outside,
-            outside,
-        ],
-        out_specs=[
-            whole(PATCH, 256),
-            pl.BlockSpec((HALF, TILE), lambda t, g: (g, t)),
-            whole(SLOTS, 256),
-            whole(SLOTS, HALF),
-        ],
+        in_specs=[pl.BlockSpec(memory_space=pltpu.SMEM)] + [vmem] * 4 + [outside] * 3,
+        out_specs=[vmem] * 4,
         scratch_shapes=[
             pltpu.VMEM((PER_HALF // PAIR, 2 * HALF, PAIR * TILE), jnp.bfloat16),
             pltpu.VMEM((PER_HALF // PAIR, CHUNK, PAIR * TILE), jnp.float32),
@@ -376,7 +368,7 @@
             pltpu.VMEM((4, HALF), jnp.int32),
             pltpu.SemaphoreType.DMA((3,)),
         ],
-        compiler_params=pltpu.CompilerParams(vmem_limit_bytes=40 * 1024 * 1024),
+        compiler_params=pltpu.CompilerParams(vmem_limit_bytes=24 * 1024 * 1024),
         name="attention",
     )(spans, queries_t, marks_f, keys_g, values_g, points, w_out, cells)
 
@@ -487,31 +479,63 @@
     spans, q_ref, qt_ref, logs_ref, do_ref, dot_ref, deltas_ref, kg_ref, vg_ref,
     dq_ref, dk_ref, dv_ref, qt, dt, qn, dn, some, slopes, dqt, dk_sum, dv_sum,
 ):
-    tile = pl.program_id(1)
+    qt[...] = jnp.zeros_like(qt)
+    dt[...] = jnp.zeros_like(dt)
+
+    def step(index, carry):
+        tile, half = index % TILES, index // TILES
+
+        @pl.when(tile == 0)
+        def _():
+            dk_sum[...] = jnp.zeros_like(dk_sum)
+            dv_sum[...] = jnp.zeros_like(dv_sum)
+
+        backward_step(
+            tile, half, spans, q_ref, qt_ref, logs_ref, do_ref, dot_ref, deltas_ref, kg_ref, vg_ref,
+            dq_ref, qt, dt, qn, dn, some, slopes, dqt, dk_sum, dv_sum,
+        )
+
+        @pl.when(tile == TILES - 1)
+        def _():
+            lanes = block_of(half, HALF)
+            dk_ref[:, lanes] = (dk_sum[:WINDOW] * 4.0).astype(jnp.bfloat16)
+            dv_ref[:, lanes] = (dv_sum[:WINDOW] * 4.0).astype(jnp.bfloat16)
+
+        return carry
+
+    lax.fori_loop(0, 2 * TILES, step, 0)
+
+
+def backward_step(
+    tile, half, spans, q_ref, qt_ref, logs_ref, do_ref, dot_ref, deltas_ref, kg_ref, vg_ref,
+    dq_ref, qt, dt, qn, dn, some, slopes, dqt, dk_sum, dv_sum,
+):
     start, count = spans[tile, 0], spans[tile, 1]
-    q_both = jnp.concatenate([qt_ref[...], logs_ref[...]], axis=0)
-    d_both = jnp.concatenate([dot_ref[...], deltas_ref[...]], axis=0)
+    mine, turned = block_of(tile, TILE), block_of(half, HALF)
+    queries, douts = q_ref[mine, turned], do_ref[mine, turned]
+    queries_t, douts_t = qt_ref[turned, mine], dot_ref[turned, mine]
+    logs, deltas = logs_ref[turned, mine], deltas_ref[turned, mine]
+    after = HALF + LOG_LANE
     for h in range(PER_HALF):
         p, place = h // PAIR, slice(h % PAIR * TILE, (h % PAIR + 1) * TILE)
-        rows = head_mask(h, 0)
-        qt[p, :, place] = q_both * rows
-        dt[p, :, place] = d_both * rows
+        own = slice(h * HEAD_SIZE, (h + 1) * HEAD_SIZE)
+        terms = head_mask(h, 0)[after : after + 32]
+        qt[p, own, place] = queries_t[own]
+        qt[p, HALF:after, place] = logs[:LOG_LANE]
+        qt[p, after : after + 32, place] = logs[LOG_LANE : LOG_LANE + 32] * terms
+        dt[p, own, place] = douts_t[own]
+        dt[p, after : after + 32, place] = deltas[LOG_LANE : LOG_LANE + 32] * terms
         lanes = head_mask(h, 1)[:, :HALF]
-        qn[p, place, :] = q_ref[...] * lanes
-        dn[p, place, :] = do_ref[...] * lanes
+        qn[p, place, :] = queries * lanes
+        dn[p, place, :] = douts * lanes
     dqt[...] = jnp.zeros_like(dqt)
-
-    @pl.when(tile == 0)
-    def _():
-        dk_sum[...] = jnp.zeros_like(dk_sum)
-        dv_sum[...] = jnp.zeros_like(dv_sum)
 
     def chunk(c, carry):
         rows = pl.ds(pl.multiple_of(start + c * CHUNK, 16), CHUNK)
-        keys_t = kg_ref[rows, :HALF].astype(jnp.float32).T.astype(jnp.bfloat16)
+        keys_t = kg_ref[half, rows, :HALF].astype(jnp.float32).T.astype(jnp.bfloat16)
         for p in range(PER_HALF // PAIR):
-            weights = jnp.exp(jnp.dot(kg_ref[rows, :], qt[p], preferred_element_type=jnp.float32))
-            dweights = jnp.dot(vg_ref[rows, :], dt[p], preferred_element_type=jnp.float32)
+            weights = jnp.exp(jnp.dot(kg_ref[half, rows, :], qt[p], preferred_element_type=jnp.float32))
+            dweights = jnp.dot(vg_ref[half, rows, :], dt[p], preferred_element_type=jnp.float32)
             place = slice(p * PAIR * TILE, (p + 1) * PAIR * TILE)
             some[:, place] = weights.astype(jnp.bfloat16)
             slopes[:, place] = (weights * dweights).astype(jnp.bfloat16)
@@ -531,31 +555,21 @@
     for h in range(PER_HALF):
         place = slice(h % PAIR * TILE, (h % PAIR + 1) * TILE)
         parts.append(dqt[h * HEAD_SIZE : (h + 1) * HEAD_SIZE, place])
-    dq_ref[...] = jnp.concatenate(parts, axis=0).T.astype(jnp.bfloat16)
-
-    @pl.when(tile == TILES - 1)
-    def _():
-        dk_ref[...] = (dk_sum[:WINDOW] * 4.0).astype(jnp.bfloat16)
-        dv_ref[...] = (dv_sum[:WINDOW] * 4.0).astype(jnp.bfloat16)
+    dq_ref[mine, turned] = jnp.concatenate(parts, axis=0).T.astype(jnp.bfloat16)
 
 
 def attend_back(spans, queries, queries_t, logs, douts, douts_t, deltas, keys_g, values_g):
-    tall = pl.BlockSpec((None, TALL, 2 * HALF), lambda g, t: (g, 0, 0))
-    mine = pl.BlockSpec((TILE, HALF), lambda g, t: (t, g))
-    turned = pl.BlockSpec((HALF, TILE), lambda g, t: (g, t))
-    sums = pl.BlockSpec((WINDOW, HALF), lambda g, t: (0, g))
+    vmem = pl.BlockSpec(memory_space=pltpu.VMEM)
     half = jnp.bfloat16
     return pl.pallas_call(
         backward_kernel,
-        grid=(2, TILES),
         out_shape=[
             jax.ShapeDtypeStruct((PATCH, 256), half),
             jax.ShapeDtypeStruct((WINDOW, 256), half),
             jax.ShapeDtypeStruct((WINDOW, 256), half),
         ],
-        in_specs=[pl.BlockSpec(memory_space=pltpu.SMEM)]
-        + [mine, turned, turned, mine, turned, turned, tall, tall],
-        out_specs=[mine, sums, sums],
+        in_specs=[pl.BlockSpec(memory_space=pltpu.SMEM)] + [vmem] * 8,
+        out_specs=[vmem] * 3,
         scratch_shapes=[
             pltpu.VMEM((PER_HALF // PAIR, 2 * HALF, PAIR * TILE), half),
             pltpu.VMEM((PER_HALF // PAIR, 2 * HALF, PAIR * TILE), half),
@@ -567,7 +581,7 @@
             pltpu.VMEM((TALL, HALF), jnp.float32),
             pltpu.VMEM((TALL, HALF), jnp.float32),
         ],
-        compiler_params=pltpu.CompilerParams(vmem_limit_bytes=40 * 1024 * 1024),
+        compiler_params=pltpu.CompilerParams(vmem_limit_bytes=24 * 1024 * 1024),
         name="attention_back",
     )(spans, queries, queries_t, logs, douts, douts_t, deltas, keys_g, values_g)
 
@@ -614,8 +628,8 @@
 def finish_kernel(
     scale, hidden, dq, dk, dv, dmixed, points, gain, w_qkv, gw_out, gw_pool, gb_pool, g_gain,
     grad_points, reduced, extras,
-    low_k, low_v, high_k, high_v, send_c, recv_c, send_x, recv_x, send_y, recv_y, recv_z,
-    gather_y, gather_x, gather_c, sems,
+    low_k, low_v, high_k, high_v, send_c, recv_c, extra_own, extra_in,
+    send_x, recv_x, send_y, recv_y, recv_z, gather_c, sems,
 ):
     me, before, after = neighbours()
     on_core, on_x, on_y, on_z = axes()
@@ -630,7 +644,12 @@
         for column in range(block.shape[1] // UNIT):
             unit = first_unit + 2 * column
             start = unit % 12 * UNIT
-            send_c[unit // 12, start : start + 2 * UNIT, :] = block[:, column * UNIT : (column + 1) * UNIT]
+            for part in range(2):
+                at = start + part * UNIT
+                rows = slice(at % X_ROWS, at % X_ROWS + UNIT)
+                send_c[unit // 12, at // X_ROWS, rows, :] = block[
+                    part * UNIT : (part + 1) * UNIT, column * UNIT : (column + 1) * UNIT
+                ]
 
     fill(gw_out[...], 12)
     fill(gw_pool[...], 16)
@@ -638,35 +657,49 @@
     pieces += [g_gain[:, i * UNIT : (i + 1) * UNIT] for i in range(4)]
     pieces += [jnp.zeros((EXTRA - 8, UNIT), jnp.float32)]
     packed = jnp.concatenate(pieces, axis=0).astype(jnp.bfloat16)
-    for r in range(2):
-        send_c[r, CORE_ROWS:, :] = packed
+    extra_own[...] = packed
     own = slice(PATCH, 2 * PATCH)
     fill((inner_rows(hidden[own, :], dq[...]) * scale).astype(jnp.bfloat16), 0)
     fill((inner_rows(hidden[...], dk[...]) * scale).astype(jnp.bfloat16), 4)
     fill((inner_rows(hidden[...], dv[...]) * scale).astype(jnp.bfloat16), 8)
 
     pl.semaphore_wait(barrier, len(greeted))
-    copies = swap(on_core, lambda r: send_c.at[r], lambda r: recv_c, sems, 0)
+    core, core_device = on_core[0], on_core[2](1 - on_core[0])
+    x, x_device = on_x[0], on_x[2]
+    quarters = [(x + k) % 4 for k in (1, 2, 3, 0)]
+    extra_copy = send(extra_own, extra_in, sems, 4, core_device)
+    core_copies = [
+        send(send_c.at[1 - core, q], recv_c.at[q], sems, k, core_device) for k, q in enumerate(quarters)
+    ]
     rims = [
-        send(dk.at[pl.ds(0, PATCH)], high_k, sems, 40, before),
-        send(dv.at[pl.ds(0, PATCH)], high_v, sems, 41, before),
-        send(dk.at[pl.ds(2 * PATCH, PATCH)], low_k, sems, 42, after),
-        send(dv.at[pl.ds(2 * PATCH, PATCH)], low_v, sems, 43, after),
+        send(dk.at[pl.ds(0, PATCH)], high_k, sems, 60, before),
+        send(dv.at[pl.ds(0, PATCH)], high_v, sems, 61, before),
+        send(dk.at[pl.ds(2 * PATCH, PATCH)], low_k, sems, 62, after),
+        send(dv.at[pl.ds(2 * PATCH, PATCH)], low_v, sems, 63, after),
     ]
+    extra_copy.wait()
+    extra = (extra_own[...].astype(jnp.float32) + extra_in[...].astype(jnp.float32)).astype(jnp.bfloat16)
+    copies = []
+    for k, q in enumerate(quarters):
+        core_copies[k].wait()
+        total = send_c[core, q].astype(jnp.float32) + recv_c[q].astype(jnp.float32)
+        if k < 3:
+            send_x[q, :X_ROWS, :] = total.astype(jnp.bfloat16)
+            send_x[q, X_ROWS:, :] = extra
+            copies.append(send(send_x.at[q], recv_x.at[x], sems, 5 + k, x_device(q)))
+        else:
+            recv_x[x, :X_ROWS, :] = total.astype(jnp.bfloat16)
+            recv_x[x, X_ROWS:, :] = extra
     dhidden = against_rows(dq[...], w_qkv[:, :256])
+    normed, inv_std = layer_stats(points[...].astype(jnp.float32))
     wait_all(copies)
-    kept = send_c.at[on_core[0]]
-    extra = (
-        kept[CORE_ROWS:, :].astype(jnp.float32) + recv_c[CORE_ROWS:, :].astype(jnp.float32)
-    ).astype(jnp.bfloat16)
-    for r in range(4):
-        rows = slice(r * X_ROWS, (r + 1) * X_ROWS)
-        total = kept[rows, :].astype(jnp.float32) + recv_c[rows, :].astype(jnp.float32)
-        send_x[r, :X_ROWS, :] = total.astype(jnp.bfloat16)
-        send_x[r, X_ROWS:, :] = extra
-
-    copies = swap(on_x, lambda r: send_x.at[r], lambda r: recv_x.at[r], sems, 1)
-    recv_x[on_x[0]] = send_x[on_x[0]]
+    extra = slot_sum(recv_x, X_ROWS, EXTRA).astype(jnp.bfloat16)
+    for r in range(8):
+        send_y[r, :Y_ROWS, :] = slot_sum(recv_x, r * Y_ROWS, Y_ROWS).astype(jnp.bfloat16)
+        send_y[r, Y_ROWS:, :] = extra
+
+    copies = swap(on_y, lambda r: send_y.at[r], lambda r: recv_y.at[r], sems, 8)
+    recv_y[on_y[0]] = send_y[on_y[0]]
     wait_all(rims)
     for columns, mine, low, high in (
         (slice(256, 512), dk, low_k, high_k), (slice(512, 768), dv, low_v, high_v)
@@ -674,29 +707,34 @@
         total = mine[own, :].astype(jnp.float32) + low[...].astype(jnp.float32)
         total = (total + high[...].astype(jnp.float32)).astype(jnp.bfloat16)
         dhidden = dhidden + against_rows(total, w_qkv[:, columns])
-    normed, inv_std = layer_stats(points[...].astype(jnp.float32))
     grad_points[...] = dmixed[...] + norm_back(dhidden * gain[...], normed, inv_std)
     wait_all(copies)
-    extra = slot_sum(recv_x, X_ROWS, EXTRA).astype(jnp.bfloat16)
-    for r in range(8):
-        send_y[r, :Y_ROWS, :] = slot_sum(recv_x, r * Y_ROWS, Y_ROWS).astype(jnp.bfloat16)
-        send_y[r, Y_ROWS:, :] = extra
-
-    copies = swap(on_y, lambda r: send_y.at[r], lambda r: recv_y.at[r], sems, 4)
-    recv_y[on_y[0]] = send_y[on_y[0]]
-    wait_all(copies)
     recv_z[on_z[0]] = slot_sum(recv_y, 0, Y_ROWS + EXTRA).astype(jnp.bfloat16)
 
-    wait_all(swap(on_z, lambda r: recv_z.at[on_z[0]], lambda r: recv_z.at[r], sems, 11))
+    wait_all(swap(on_z, lambda r: recv_z.at[on_z[0]], lambda r: recv_z.at[r], sems, 15))
     total = slot_sum(recv_z, 0, Y_ROWS + EXTRA)
     extras[...] = total[Y_ROWS:]
-    gather_y[on_y[0]] = total[:Y_ROWS].astype(jnp.bfloat16)
-    wait_all(swap(on_y, lambda r: gather_y.at[on_y[0]], lambda r: gather_y.at[r], sems, 18))
-    gather_x[on_x[0]] = gather_y[...]
-    copies = swap(on_x, lambda r: gather_y, lambda r: gather_x.at[r], sems, 25)
-    wait_all(copies)
-    gather_c[on_core[0]] = gather_x[...]
-    wait_all(swap(on_core, lambda r: gather_x, lambda r: gather_c.at[r], sems, 28))
+    y, y_device = on_y[0], on_y[2]
+    gather_c[core, x, y] = total[:Y_ROWS].astype(jnp.bfloat16)
+    order = (1, 7, 2, 6, 3, 5, 4)
+
+    def pass_on(k):
+        piece = gather_c.at[core, x, (y + 8 - k) % 8]
+        return [send(piece, piece, sems, 29 + 3 * k + i - 1, x_device((x + i) % 4)) for i in range(1, 4)]
+
+    mine = gather_c.at[core, x, y]
+    y_copies = {k: send(mine, mine, sems, 22 + k - 1, y_device((y + k) % 8)) for k in order}
+    x_copies = {0: pass_on(0)}
+    for k in order:
+        y_copies[k].wait()
+        x_copies[k] = pass_on(k)
+    core_copies = [send(gather_c.at[core, x], gather_c.at[core, x], sems, 53, core_device)]
+    for i in range(1, 4):
+        for k in (0,) + order:
+            x_copies[k][i - 1].wait()
+        slot = gather_c.at[core, (x + 4 - i) % 4]
+        core_copies.append(send(slot, slot, sems, 53 + i, core_device))
+    wait_all(core_copies)
     for c in range(2):
         for r in range(4):
             for s in range(8):
@@ -726,17 +764,17 @@
         out_specs=[vmem] * 3,
         scratch_shapes=[pltpu.VMEM((PATCH, 256), half)] * 4
         + [
-            pltpu.VMEM((2, CORE_ROWS + EXTRA, UNIT), half),
-            pltpu.VMEM((CORE_ROWS + EXTRA, UNIT), half),
+            pltpu.VMEM((2, 4, X_ROWS, UNIT), half),
+            pltpu.VMEM((4, X_ROWS, UNIT), half),
+            pltpu.VMEM((EXTRA, UNIT), half),
+            pltpu.VMEM((EXTRA, UNIT), half),
             pltpu.VMEM((4, X_ROWS + EXTRA, UNIT), half),
             pltpu.VMEM((4, X_ROWS + EXTRA, UNIT), half),
             pltpu.VMEM((8, Y_ROWS + EXTRA, UNIT), half),
             pltpu.VMEM((8, Y_ROWS + EXTRA, UNIT), half),
             pltpu.VMEM((8, Y_ROWS + EXTRA, UNIT), half),
-            pltpu.VMEM((8, Y_ROWS, UNIT), half),
-            pltpu.VMEM((4, 8, Y_ROWS, UNIT), half),
             pltpu.VMEM((2, 4, 8, Y_ROWS, UNIT), half),
-            pltpu.SemaphoreType.DMA((2, 44)),
+            pltpu.SemaphoreType.DMA((2, 64)),
         ],
         compiler_params=pltpu.CompilerParams(
             collective_id=3, has_side_effects=True, vmem_limit_bytes=40 * 1024 * 1024

time: 111 us -> 106 us (0.955)
  Pallas kernels: 109 us -> 105 us
    pallas_call x2, Pallas kernels: 31.9 us -> 24.5 us  [the longest x1 14.7 us: attend_back(): pl.pallas_call(backward_kernel, out_shape=[jax.ShapeDtypeStruct((PATCH, 2...]
    pallas_call x1, Pallas kernels: 43.4 us -> 45.9 us  [finish(): pl.pallas_call(functools.partial(finish_kernel, scale), out_shape=[jax.Sh...]
where the time goes in v2:
time: 106 us; the launch traced here: 105 us
  Pallas kernels  105 us (99%)
    pallas_call x1, Pallas kernels, finish(): pl.pallas_call(functools.partial(finish_kernel, scale), out_shape=[jax.Sh...  45.9 us
    pallas_call x1, Pallas kernels, prepare(): pl.pallas_call(prepare_kernel, out_shape=[jax.ShapeDtypeStruct((PATCH, 25...  18.8 us
    pallas_call x1, Pallas kernels, attend_back(): pl.pallas_call(backward_kernel, out_shape=[jax.ShapeDtypeStruct((PATCH, 2...  14.7 us
    pallas_call x1, Pallas kernels, pool(): pl.pallas_call(functools.partial(pool_kernel, scale), out_shape=[jax.Shap...  13.4 us
    pallas_call x1, Pallas kernels, attend(): pl.pallas_call(forward_kernel, out_shape=[jax.ShapeDtypeStruct((PATCH, 25...  9.8 us

profile of v2, /device:TPU:1, one launch (start us, length us, event | category | flops | bytes accessed | tf_op | source)
XLA Modules:
  0.0 105.5 jit_solution(5322508211822932851)
XLA Ops:
  0.6 18.8 %prepare.1 = (bf16[512,256]{1,0:T(8,128)(2,1)S(1)}, bf16[256,512]{1,0:T(8,128)(2,1)S(1)}, bf16[2,1584,256]{2,1,0:T(8,128)(2,1)S(1)}, bf16[2,1584,256]{2,1,0:T(8,...) custom-call(bf16[512,256]{1,0:T(8,128)(2,1)} %points.1, ...), custom_call_target="tpu_custom_call" | custom-call | tf_op jit(solution)/shard_map/prepare/pallas_call | solution.py:203
  19.5 0.0 copy-start.2
  19.5 0.0 copy-start.3
  19.5 0.0 copy-start.4
  19.5 0.0 copy-start.5
  19.5 0.0 copy-start.7
  19.5 0.0 copy-start.8
  19.5 9.8 %attention.1 = (bf16[512,256]{1,0:T(8,128)(2,1)S(1)}, bf16[256,512]{1,0:T(8,128)(2,1)S(1)}, f32[144,256]{1,0:T(8,128)S(1)}, f32[144,128]{1,0:T(8,128)S(1)}) custom-call(s32[4,2]{1,0:T(4,128)S(1)} %get-tuple-element.40.spans, bf16[256,512]{1,0:T(8,128)(2,1)S(1)} %get-tuple-element.42.qt_ref, bf16[128,512]{1,0:T(8,128)(2,1)S(1)} %get-tuple-element.43.f_ref, ...), custom_call_target="tpu_custom_call" | custom-call | tf_op jit(solution)/shard_map/attention/pallas_call | solution.py:350
  29.3 0.0 copy-done.2
  29.3 0.0 copy-done.3
  29.4 0.0 copy-done.4
  29.4 0.0 copy-done.5
  29.4 0.0 copy-done.7
  29.4 0.0 copy-done.8
  29.4 13.4 %pooling.1 = (f32[512,256]{1,0:T(8,128)S(1)}, bf16[512,256]{1,0:T(8,128)(2,1)S(1)}, bf16[256,512]{1,0:T(8,128)(2,1)S(1)}, bf16[256,512]{1,0:T(8,128)(2,1)S(1)}, ...) custom-call(f32[144,256]{1,0:T(8,128)S(1)} %get-tuple-element.47.sums,, ...), custom_call_target="tpu_custom_call" | custom-call | tf_op jit(solution)/shard_map/pooling/pallas_call | solution.py:450
  42.8 0.0 copy-start
  42.9 0.0 copy-start.1
  42.9 0.0 copy-start.6
  42.9 14.7 %attention_back.1 = (bf16[512,256]{1,0:T(8,128)(2,1)S(1)}, bf16[1536,256]{1,0:T(8,128)(2,1)S(1)}, bf16[1536,256]{1,0:T(8,128)(2,1)S(1)}) custom-call(s32[4,2]{1,0:T(4,128)S(1)} %get-tuple-element.40.spans, bf16[512,256]{1,0:T(8,128)(2,1)S(1)} %get-tuple-element.41.q_ref, bf16[256,512]{1,0:T(8,128)(2,1)S(1)} %get-tuple-element.42.qt_ref, ...), custom_call_target="tpu_custom_call" | custom-call | tf_op jit(solution)/shard_map/attention_back/pallas_call | solution.py:564
  57.5 0.0 copy-done
  57.5 0.0 copy-done.1
  57.6 0.0 copy-done.6
  57.6 45.9 %finish.1 = (f32[512,256]{1,0:T(8,128)S(1)}, bf16[3072,128]{1,0:T(8,128)(2,1)S(1)}, f32[16,128]{1,0:T(8,128)S(1)}) custom-call(bf16[1536,256]{1,0:T(8,128)(2,1)S(1)} %get-tuple-element.39.hidden, bf16[512,256]{1,0:T(8,128)(2,1)S(1)} %get-tuple-element.53.dq, bf16[1536,256]{1,0:T(8,128)(2,1)S(1)} %get-tuple-element.54.dk, ...), custom_call_target="tpu_custom_call" | custom-call | tf_op jit(solution)/shard_map/finish/pallas_call | solution.py:756
  103.5 1.9 %unpack.1 = (f32[256,768]{1,0:T(8,128)}, f32[256,256]{1,0:T(8,128)}, f32[1,256]{1,0:T(1,128)}, f32[256,512]{1,0:T(8,128)}, f32[1,512]{1,0:T(1,128)}, /*index=5*/f32[1,512]{1,0:T(1,128)}, f32[512,256]{1,0:T(8,128)}) custom-call(bf16[3072,128]{1,0:T(8,128)(2,1)S(1)} %get-tuple-element.61.reduced, f32[16,128]{1,0:T(8,128)S(1)} %get-tuple-element.62.extras, ...), custom_call_target="tpu_custom_call" | custom-call | tf_op jit(solution)/shard_map/unpack/pallas_call | solution.py:809
Async XLA Ops:
  19.5 9.9 %copy-start.2 = (bf16[256,256]{1,0:T(8,128)(2,1)S(1)}, bf16[256,256]{1,0:T(8,128)(2,1)}, u32[]{:S(2)}) copy-start(bf16[256,256]{1,0:T(8,128)(2,1)} %w_out.1) | copy-start | bytes 393220
  19.5 9.9 %copy-start.3 = (bf16[256,512]{1,0:T(8,128)(2,1)S(1)}, bf16[256,512]{1,0:T(8,128)(2,1)}, u32[]{:S(2)}) copy-start(bf16[256,512]{1,0:T(8,128)(2,1)} %w_pool.1) | copy-start | bytes 786436
  19.5 9.9 %copy-start.4 = (f32[128,512]{1,0:T(8,128)S(1)}, f32[128,512]{1,0:T(8,128)}, u32[]{:S(2)}) copy-start(f32[128,512]{1,0:T(8,128)} %cotangent.1) | copy-start | bytes 786436
  19.5 9.9 %copy-start.5 = (s32[512]{0:T(512)S(1)}, s32[512]{0:T(512)}, u32[]{:S(2)}) copy-start(s32[512]{0:T(512)} %param.12) | copy-start | bytes 6148
  19.5 9.9 %copy-start.7 = (f32[512]{0:T(512)S(1)}, f32[512]{0:T(512)}, u32[]{:S(2)}) copy-start(f32[512]{0:T(512)} %param.17) | copy-start | bytes 6148
  19.5 9.9 %copy-start.8 = (f32[512]{0:T(512)S(1)}, f32[512]{0:T(512)}, u32[]{:S(2)}) copy-start(f32[512]{0:T(512)} %param.18) | copy-start | bytes 6148
  42.8 14.7 %copy-start = (bf16[512,256]{1,0:T(8,128)(2,1)S(1)}, bf16[512,256]{1,0:T(8,128)(2,1)}, u32[]{:S(2)}) copy-start(bf16[512,256]{1,0:T(8,128)(2,1)} %points.1) | copy-start | bytes 786436
  42.9 14.7 %copy-start.1 = (bf16[256,768]{1,0:T(8,128)(2,1)S(1)}, bf16[256,768]{1,0:T(8,128)(2,1)}, u32[]{:S(2)}) copy-start(bf16[256,768]{1,0:T(8,128)(2,1)} %w_qkv.1) | copy-start | bytes 1179652
  42.9 14.7 %copy-start.6 = (f32[256]{0:T(256)S(1)}, f32[256]{0:T(256)}, u32[]{:S(2)}) copy-start(f32[256]{0:T(256)} %param.13) | copy-start | bytes 3076

commit v3 on v2

--- a/solution.py
+++ b/solution.py
@@ -272,12 +272,12 @@
 
     def step(index, carry):
         forward_step(
-            index // 2, index % 2, spans, qt_ref, f_ref, kg_ref, vg_ref, att_ref, logs_ref,
+            index, spans, qt_ref, f_ref, kg_ref, vg_ref, att_ref, logs_ref,
             qt, kept, att_t, top_t, total_t,
         )
         return carry
 
-    lax.fori_loop(0, 2 * TILES, step, 0)
+    lax.fori_loop(0, TILES, step, 0)
     for copy in late:
         copy.wait()
     mixed = points[...].astype(jnp.float32) + jnp.dot(
@@ -290,58 +290,65 @@
     counts_ref[...] = jnp.broadcast_to(jnp.sum(member, axis=1, keepdims=True), (SLOTS, HALF))
 
 
+PAIRS = PER_HALF // PAIR
+
+
 def forward_step(
-    tile, half, spans, qt_ref, f_ref, kg_ref, vg_ref, att_ref, logs_ref, qt, kept, att_t, top_t, total_t
+    tile, spans, qt_ref, f_ref, kg_ref, vg_ref, att_ref, logs_ref, qt, kept, att_t, top_t, total_t
 ):
     start, count = spans[tile, 0], spans[tile, 1]
-    mine, turned = block_of(tile, TILE), block_of(half, HALF)
-    queries_t, marks = qt_ref[turned, mine], f_ref[:LOG_LANE, mine]
-    for h in range(PER_HALF):
-        place = slice(h % PAIR * TILE, (h % PAIR + 1) * TILE)
-        own = slice(h * HEAD_SIZE, (h + 1) * HEAD_SIZE)
-        qt[h // PAIR, own, place] = queries_t[own]
-        qt[h // PAIR, HALF : HALF + LOG_LANE, place] = marks
+    mine = block_of(tile, TILE)
+    marks = f_ref[:LOG_LANE, mine]
+    for half in range(2):
+        queries_t = qt_ref[half * HALF : (half + 1) * HALF, mine]
+        for h in range(PER_HALF):
+            p, place = half * PAIRS + h // PAIR, slice(h % PAIR * TILE, (h % PAIR + 1) * TILE)
+            own = slice(h * HEAD_SIZE, (h + 1) * HEAD_SIZE)
+            qt[p, own, place] = queries_t[own]
+            qt[p, HALF : HALF + LOG_LANE, place] = marks
     top_t[...] = jnp.full_like(top_t, -3e38)
     total_t[...] = jnp.zeros_like(total_t)
     att_t[...] = jnp.zeros_like(att_t)
 
     def chunk(c, carry):
         rows = pl.ds(pl.multiple_of(start + c * CHUNK, 16), CHUNK)
-        values_t = vg_ref[half, rows, :HALF].astype(jnp.float32).T.astype(jnp.bfloat16)
         ones = jnp.ones((16, CHUNK), jnp.bfloat16)
-        tops = []
-        for p in range(PER_HALF // PAIR):
-            scores = jnp.dot(kg_ref[half, rows, :], qt[p], preferred_element_type=jnp.float32)
-            kept[p] = scores
-            tops.append(jnp.maximum(top_t[p : p + 1, :], tall_max(scores)))
-        for p in range(PER_HALF // PAIR):
+        tops, values_t = [], []
+        for half in range(2):
+            values_t.append(vg_ref[half, rows, :HALF].astype(jnp.float32).T.astype(jnp.bfloat16))
+            for p in range(half * PAIRS, (half + 1) * PAIRS):
+                scores = jnp.dot(kg_ref[half, rows, :], qt[p], preferred_element_type=jnp.float32)
+                kept[p] = scores
+                tops.append(jnp.maximum(top_t[p : p + 1, :], tall_max(scores)))
+        for p in range(2 * PAIRS):
             before, top = top_t[p : p + 1, :], tops[p]
             weights = jnp.exp(kept[p] - top).astype(jnp.bfloat16)
             decay = jnp.exp(before - top)
             top_t[p : p + 1, :] = top
-            own = slice(p * PAIR * HEAD_SIZE, (p + 1) * PAIR * HEAD_SIZE)
-            left = jnp.concatenate([values_t[own], ones], axis=0)
+            size = PAIR * HEAD_SIZE
+            own, inner = slice(p * size, (p + 1) * size), slice(p % PAIRS * size, (p % PAIRS + 1) * size)
+            left = jnp.concatenate([values_t[p // PAIRS][inner], ones], axis=0)
             mixed = jnp.dot(left, weights, preferred_element_type=jnp.float32)
-            count_rows = PAIR * HEAD_SIZE
-            total_t[p : p + 1, :] = total_t[p : p + 1, :] * decay + mixed[count_rows : count_rows + 1]
-            att_t[own, :] = att_t[own, :] * decay + mixed[:count_rows]
+            total_t[p : p + 1, :] = total_t[p : p + 1, :] * decay + mixed[size : size + 1]
+            att_t[own, :] = att_t[own, :] * decay + mixed[:size]
         return carry
 
     lax.fori_loop(0, count, chunk, 0)
     logs_p = -(top_t[...] + jnp.log(total_t[...]))
-    parts, logs = [], []
-    for h in range(PER_HALF):
-        p, columns = h // PAIR, slice(h % PAIR * TILE, (h % PAIR + 1) * TILE)
-        piece = att_t[h * HEAD_SIZE : (h + 1) * HEAD_SIZE, columns]
-        parts.append(piece / total_t[p : p + 1, columns])
-        logs.append(logs_p[p : p + 1, columns])
-    attended = jnp.concatenate(parts, axis=0).T.astype(jnp.bfloat16)
-    att_ref[mine, turned] = attended
-    logs = jnp.concatenate(logs, axis=0)
-    terms = [split_three(logs, i) for i in range(3)]
     spare = jnp.zeros((HALF - LOG_LANE - 24, TILE), jnp.float32)
-    ending = jnp.concatenate(terms + [spare], axis=0).astype(jnp.bfloat16)
-    logs_ref[turned, mine] = jnp.concatenate([marks, ending], axis=0)
+    for half in range(2):
+        parts, logs = [], []
+        for h in range(half * PER_HALF, (half + 1) * PER_HALF):
+            p, columns = h // PAIR, slice(h % PAIR * TILE, (h % PAIR + 1) * TILE)
+            piece = att_t[h * HEAD_SIZE : (h + 1) * HEAD_SIZE, columns]
+            parts.append(piece / total_t[p : p + 1, columns])
+            logs.append(logs_p[p : p + 1, columns])
+        lanes = slice(half * HALF, (half + 1) * HALF)
+        att_ref[mine, lanes] = jnp.concatenate(parts, axis=0).T.astype(jnp.bfloat16)
+        logs = jnp.concatenate(logs, axis=0)
+        terms = [split_three(logs, i) for i in range(3)]
+        ending = jnp.concatenate(terms + [spare], axis=0).astype(jnp.bfloat16)
+        logs_ref[lanes, mine] = jnp.concatenate([marks, ending], axis=0)
 
 
 def attend(spans, queries_t, marks_f, keys_g, values_g, points, w_out, cells):
@@ -358,11 +365,11 @@
         in_specs=[pl.BlockSpec(memory_space=pltpu.SMEM)] + [vmem] * 4 + [outside] * 3,
         out_specs=[vmem] * 4,
         scratch_shapes=[
-            pltpu.VMEM((PER_HALF // PAIR, 2 * HALF, PAIR * TILE), jnp.bfloat16),
-            pltpu.VMEM((PER_HALF // PAIR, CHUNK, PAIR * TILE), jnp.float32),
-            pltpu.VMEM((HALF, PAIR * TILE), jnp.float32),
-            pltpu.VMEM((PER_HALF // PAIR, PAIR * TILE), jnp.float32),
-            pltpu.VMEM((PER_HALF // PAIR, PAIR * TILE), jnp.float32),
+            pltpu.VMEM((2 * PAIRS, 2 * HALF, PAIR * TILE), jnp.bfloat16),
+            pltpu.VMEM((2 * PAIRS, CHUNK, PAIR * TILE), jnp.float32),
+            pltpu.VMEM((2 * HALF, PAIR * TILE), jnp.float32),
+            pltpu.VMEM((2 * PAIRS, PAIR * TILE), jnp.float32),
+            pltpu.VMEM((2 * PAIRS, PAIR * TILE), jnp.float32),
             pltpu.VMEM((PATCH, 256), jnp.bfloat16),
             pltpu.VMEM((256, 256), jnp.bfloat16),
             pltpu.VMEM((4, HALF), jnp.int32),
@@ -481,81 +488,87 @@
 ):
     qt[...] = jnp.zeros_like(qt)
     dt[...] = jnp.zeros_like(dt)
-
-    def step(index, carry):
-        tile, half = index % TILES, index // TILES
-
-        @pl.when(tile == 0)
-        def _():
-            dk_sum[...] = jnp.zeros_like(dk_sum)
-            dv_sum[...] = jnp.zeros_like(dv_sum)
-
+    dk_sum[...] = jnp.zeros_like(dk_sum)
+    dv_sum[...] = jnp.zeros_like(dv_sum)
+
+    def step(tile, carry):
         backward_step(
-            tile, half, spans, q_ref, qt_ref, logs_ref, do_ref, dot_ref, deltas_ref, kg_ref, vg_ref,
+            tile, spans, q_ref, qt_ref, logs_ref, do_ref, dot_ref, deltas_ref, kg_ref, vg_ref,
             dq_ref, qt, dt, qn, dn, some, slopes, dqt, dk_sum, dv_sum,
         )
-
-        @pl.when(tile == TILES - 1)
-        def _():
-            lanes = block_of(half, HALF)
-            dk_ref[:, lanes] = (dk_sum[:WINDOW] * 4.0).astype(jnp.bfloat16)
-            dv_ref[:, lanes] = (dv_sum[:WINDOW] * 4.0).astype(jnp.bfloat16)
-
         return carry
 
-    lax.fori_loop(0, 2 * TILES, step, 0)
+    lax.fori_loop(0, TILES, step, 0)
+    dk_ref[...] = (dk_sum[:WINDOW] * 4.0).astype(jnp.bfloat16)
+    dv_ref[...] = (dv_sum[:WINDOW] * 4.0).astype(jnp.bfloat16)
 
 
 def backward_step(
-    tile, half, spans, q_ref, qt_ref, logs_ref, do_ref, dot_ref, deltas_ref, kg_ref, vg_ref,
+    tile, spans, q_ref, qt_ref, logs_ref, do_ref, dot_ref, deltas_ref, kg_ref, vg_ref,
     dq_ref, qt, dt, qn, dn, some, slopes, dqt, dk_sum, dv_sum,
 ):
     start, count = spans[tile, 0], spans[tile, 1]
-    mine, turned = block_of(tile, TILE), block_of(half, HALF)
-    queries, douts = q_ref[mine, turned], do_ref[mine, turned]
-    queries_t, douts_t = qt_ref[turned, mine], dot_ref[turned, mine]
-    logs, deltas = logs_ref[turned, mine], deltas_ref[turned, mine]
+    mine = block_of(tile, TILE)
     after = HALF + LOG_LANE
-    for h in range(PER_HALF):
-        p, place = h // PAIR, slice(h % PAIR * TILE, (h % PAIR + 1) * TILE)
-        own = slice(h * HEAD_SIZE, (h + 1) * HEAD_SIZE)
-        terms = head_mask(h, 0)[after : after + 32]
-        qt[p, own, place] = queries_t[own]
-        qt[p, HALF:after, place] = logs[:LOG_LANE]
-        qt[p, after : after + 32, place] = logs[LOG_LANE : LOG_LANE + 32] * terms
-        dt[p, own, place] = douts_t[own]
-        dt[p, after : after + 32, place] = deltas[LOG_LANE : LOG_LANE + 32] * terms
-        lanes = head_mask(h, 1)[:, :HALF]
-        qn[p, place, :] = queries * lanes
-        dn[p, place, :] = douts * lanes
+    halves = [slice(half * HALF, (half + 1) * HALF) for half in range(2)]
+    for half, turned in enumerate(halves):
+        queries, douts = q_ref[mine, turned], do_ref[mine, turned]
+        queries_t, douts_t = qt_ref[turned, mine], dot_ref[turned, mine]
+        logs, deltas = logs_ref[turned, mine], deltas_ref[turned, mine]
+        for h in range(PER_HALF):
+            p, place = half * PAIRS + h // PAIR, slice(h % PAIR * TILE, (h % PAIR + 1) * TILE)
+            own = slice(h * HEAD_SIZE, (h + 1) * HEAD_SIZE)
+            terms = head_mask(h, 0)[after : after + 32]
+            qt[p, own, place] = queries_t[own]
+            qt[p, HALF:after, place] = logs[:LOG_LANE]
+            qt[p, after : after + 32, place] = logs[LOG_LANE : LOG_LANE + 32] * terms
+            dt[p, own, place] = douts_t[own]
+            dt[p, after : after + 32, place] = deltas[LOG_LANE : LOG_LANE + 32] * terms
+            lanes = head_mask(h, 1)[:, :HALF]
+            qn[p, place, :] = queries * lanes
+            dn[p, place, :] = douts * lanes
     dqt[...] = jnp.zeros_like(dqt)
+    width = PAIR * TILE
 
     def chunk(c, carry):
         rows = pl.ds(pl.multiple_of(start + c * CHUNK, 16), CHUNK)
-        keys_t = kg_ref[half, rows, :HALF].astype(jnp.float32).T.astype(jnp.bfloat16)
-        for p in range(PER_HALF // PAIR):
-            weights = jnp.exp(jnp.dot(kg_ref[half, rows, :], qt[p], preferred_element_type=jnp.float32))
-            dweights = jnp.dot(vg_ref[half, rows, :], dt[p], preferred_element_type=jnp.float32)
-            place = slice(p * PAIR * TILE, (p + 1) * PAIR * TILE)
-            some[:, place] = weights.astype(jnp.bfloat16)
-            slopes[:, place] = (weights * dweights).astype(jnp.bfloat16)
-        depth = PER_HALF * TILE
-        dk = jnp.dot(slopes[...], qn[...].reshape(depth, HALF), preferred_element_type=jnp.float32)
-        dv = jnp.dot(some[...], dn[...].reshape(depth, HALF), preferred_element_type=jnp.float32)
-        for p in range(PER_HALF // PAIR):
-            own = slice(p * PAIR * HEAD_SIZE, (p + 1) * PAIR * HEAD_SIZE)
-            place = slice(p * PAIR * TILE, (p + 1) * PAIR * TILE)
-            dqt[own, :] += jnp.dot(keys_t[own], slopes[:, place], preferred_element_type=jnp.float32)
-        dk_sum[rows, :] += dk
-        dv_sum[rows, :] += dv
+        keys_t = []
+        for half in range(2):
+            keys_t.append(kg_ref[half, rows, :HALF].astype(jnp.float32).T.astype(jnp.bfloat16))
+            for p in range(half * PAIRS, (half + 1) * PAIRS):
+                weights = jnp.exp(
+                    jnp.dot(kg_ref[half, rows, :], qt[p], preferred_element_type=jnp.float32)
+                )
+                dweights = jnp.dot(vg_ref[half, rows, :], dt[p], preferred_element_type=jnp.float32)
+                place = slice(p * width, (p + 1) * width)
+                some[:, place] = weights.astype(jnp.bfloat16)
+                slopes[:, place] = (weights * dweights).astype(jnp.bfloat16)
+        depth = PAIRS * width
+        for half, lanes in enumerate(halves):
+            place, pairs = slice(half * depth, (half + 1) * depth), slice(half * PAIRS, (half + 1) * PAIRS)
+            dk_sum[rows, lanes] += jnp.dot(
+                slopes[:, place], qn[pairs].reshape(depth, HALF), preferred_element_type=jnp.float32
+            )
+            dv_sum[rows, lanes] += jnp.dot(
+                some[:, place], dn[pairs].reshape(depth, HALF), preferred_element_type=jnp.float32
+            )
+        size = PAIR * HEAD_SIZE
+        for p in range(2 * PAIRS):
+            inner = slice(p % PAIRS * size, (p % PAIRS + 1) * size)
+            dqt[p * size : (p + 1) * size, :] += jnp.dot(
+                keys_t[p // PAIRS][inner],
+                slopes[:, p * width : (p + 1) * width],
+                preferred_element_type=jnp.float32,
+            )
         return carry
 
     lax.fori_loop(0, count, chunk, 0)
-    parts = []
-    for h in range(PER_HALF):
-        place = slice(h % PAIR * TILE, (h % PAIR + 1) * TILE)
-        parts.append(dqt[h * HEAD_SIZE : (h + 1) * HEAD_SIZE, place])
-    dq_ref[mine, turned] = jnp.concatenate(parts, axis=0).T.astype(jnp.bfloat16)
+    for half, turned in enumerate(halves):
+        parts = []
+        for h in range(half * PER_HALF, (half + 1) * PER_HALF):
+            place = slice(h % PAIR * TILE, (h % PAIR + 1) * TILE)
+            parts.append(dqt[h * HEAD_SIZE : (h + 1) * HEAD_SIZE, place])
+        dq_ref[mine, turned] = jnp.concatenate(parts, axis=0).T.astype(jnp.bfloat16)
 
 
 def attend_back(spans, queries, queries_t, logs, douts, douts_t, deltas, keys_g, values_g):
@@ -571,15 +584,15 @@
         in_specs=[pl.BlockSpec(memory_space=pltpu.SMEM)] + [vmem] * 8,
         out_specs=[vmem] * 3,
         scratch_shapes=[
-            pltpu.VMEM((PER_HALF // PAIR, 2 * HALF, PAIR * TILE), half),
-            pltpu.VMEM((PER_HALF // PAIR, 2 * HALF, PAIR * TILE), half),
-            pltpu.VMEM((PER_HALF // PAIR, PAIR * TILE, HALF), half),
-            pltpu.VMEM((PER_HALF // PAIR, PAIR * TILE, HALF), half),
-            pltpu.VMEM((CHUNK, 256 * PER_HALF // PAIR), half),
-            pltpu.VMEM((CHUNK, 256 * PER_HALF // PAIR), half),
-            pltpu.VMEM((HALF, PAIR * TILE), jnp.float32),
-            pltpu.VMEM((TALL, HALF), jnp.float32),
-            pltpu.VMEM((TALL, HALF), jnp.float32),
+            pltpu.VMEM((2 * PAIRS, 2 * HALF, PAIR * TILE), half),
+            pltpu.VMEM((2 * PAIRS, 2 * HALF, PAIR * TILE), half),
+            pltpu.VMEM((2 * PAIRS, PAIR * TILE, HALF), half),
+            pltpu.VMEM((2 * PAIRS, PAIR * TILE, HALF), half),
+            pltpu.VMEM((CHUNK, 2 * PAIRS * PAIR * TILE), half),
+            pltpu.VMEM((CHUNK, 2 * PAIRS * PAIR * TILE), half),
+            pltpu.VMEM((2 * HALF, PAIR * TILE), jnp.float32),
+            pltpu.VMEM((TALL, 2 * HALF), jnp.float32),
+            pltpu.VMEM((TALL, 2 * HALF), jnp.float32),
         ],
         compiler_params=pltpu.CompilerParams(vmem_limit_bytes=24 * 1024 * 1024),
         name="attention_back",
@@ -604,13 +617,17 @@
     )
 
 
+def far_first(size):
+    return sorted(range(1, size), key=lambda k: -min(k, size - k))
+
+
 def swap(axis, source, landing, sems, first):
     rank, size, device = axis
     copies = []
-    for k in range(1, size):
+    for k in far_first(size):
         peer = (rank + k) % size
         copies.append(send(source(peer), landing(rank), sems, first + k - 1, device(peer)))
-    return copies
+    return copies[::-1]
 
 
 def wait_all(copies):
@@ -634,9 +651,10 @@
     me, before, after = neighbours()
     on_core, on_x, on_y, on_z = axes()
     barrier = pltpu.get_barrier_semaphore()
-    greeted = [before, after]
-    for rank, size, device in (on_core, on_x, on_y, on_z):
-        greeted += [device((rank + k) % size) for k in range(1, size)]
+    greeted = []
+    for rank, size, device in (on_z, on_y, on_x, on_core):
+        greeted += [device((rank + k) % size) for k in far_first(size)]
+    greeted += [before, after]
     for device in greeted:
         pl.semaphore_signal(barrier, inc=1, device_id=(device,), device_id_type=MESH)
 
@@ -666,8 +684,9 @@
     pl.semaphore_wait(barrier, len(greeted))
     core, core_device = on_core[0], on_core[2](1 - on_core[0])
     x, x_device = on_x[0], on_x[2]
-    quarters = [(x + k) % 4 for k in (1, 2, 3, 0)]
-    extra_copy = send(extra_own, extra_in, sems, 4, core_device)
+    steps = (2, 1, 3, 0)
+    quarters = [(x + k) % 4 for k in steps]
+    extra_copy = send(extra_own, extra_in, sems, 57, core_device)
     core_copies = [
         send(send_c.at[1 - core, q], recv_c.at[q], sems, k, core_device) for k, q in enumerate(quarters)
     ]
@@ -686,7 +705,7 @@
         if k < 3:
             send_x[q, :X_ROWS, :] = total.astype(jnp.bfloat16)
             send_x[q, X_ROWS:, :] = extra
-            copies.append(send(send_x.at[q], recv_x.at[x], sems, 5 + k, x_device(q)))
+            copies.append(send(send_x.at[q], recv_x.at[x], sems, 4 + steps[k], x_device(q)))
         else:
             recv_x[x, :X_ROWS, :] = total.astype(jnp.bfloat16)
             recv_x[x, X_ROWS:, :] = extra
@@ -720,18 +739,18 @@
 
     def pass_on(k):
         piece = gather_c.at[core, x, (y + 8 - k) % 8]
-        return [send(piece, piece, sems, 29 + 3 * k + i - 1, x_device((x + i) % 4)) for i in range(1, 4)]
+        return {i: send(piece, piece, sems, 28 + 3 * k + i, x_device((x + i) % 4)) for i in (2, 1, 3)}
 
     mine = gather_c.at[core, x, y]
-    y_copies = {k: send(mine, mine, sems, 22 + k - 1, y_device((y + k) % 8)) for k in order}
+    y_copies = {k: send(mine, mine, sems, 22 + k - 1, y_device((y + k) % 8)) for k in order[::-1]}
     x_copies = {0: pass_on(0)}
     for k in order:
         y_copies[k].wait()
         x_copies[k] = pass_on(k)
     core_copies = [send(gather_c.at[core, x], gather_c.at[core, x], sems, 53, core_device)]
-    for i in range(1, 4):
+    for i in (1, 3, 2):
         for k in (0,) + order:
-            x_copies[k][i - 1].wait()
+            x_copies[k][i].wait()
         slot = gather_c.at[core, (x + 4 - i) % 4]
         core_copies.append(send(slot, slot, sems, 53 + i, core_device))
     wait_all(core_copies)

time: 106 us -> 99.3 us (0.937)
  Pallas kernels: 105 us -> 98.3 us
    pallas_call x1, Pallas kernels: 45.9 us -> 37.8 us  [finish(): pl.pallas_call(functools.partial(finish_kernel, scale), out_shape=[jax.Sh...]
    pallas_call x1, Pallas kernels: 14.7 us -> 16.4 us  [attend_back(): pl.pallas_call(backward_kernel, out_shape=[jax.ShapeDtypeStruct((PATCH, 2...]
where the time goes in v3:
time: 99.3 us; the launch traced here: 99.2 us
  Pallas kernels  98.3 us (99%)
    pallas_call x1, Pallas kernels, finish(): pl.pallas_call(functools.partial(finish_kernel, scale), out_shape=[jax.Sh...  37.8 us
    pallas_call x1, Pallas kernels, prepare(): pl.pallas_call(prepare_kernel, out_shape=[jax.ShapeDtypeStruct((PATCH, 25...  18.8 us
    pallas_call x1, Pallas kernels, attend_back(): pl.pallas_call(backward_kernel, out_shape=[jax.ShapeDtypeStruct((PATCH, 2...  16.4 us
    pallas_call x1, Pallas kernels, pool(): pl.pallas_call(functools.partial(pool_kernel, scale), out_shape=[jax.Shap...  13.4 us
    pallas_call x1, Pallas kernels, attend(): pl.pallas_call(forward_kernel, out_shape=[jax.ShapeDtypeStruct((PATCH, 25...  9.99 us

profile of v3, /device:TPU:1, one launch (start us, length us, event | category | flops | bytes accessed | tf_op | source)
XLA Modules:
  0.0 99.2 jit_solution(10414506634641113382)
XLA Ops:
  0.6 18.8 %prepare.1 = (bf16[512,256]{1,0:T(8,128)(2,1)S(1)}, bf16[256,512]{1,0:T(8,128)(2,1)S(1)}, bf16[2,1584,256]{2,1,0:T(8,128)(2,1)S(1)}, bf16[2,1584,256]{2,1,0:T(8,...) custom-call(bf16[512,256]{1,0:T(8,128)(2,1)} %points.1, ...), custom_call_target="tpu_custom_call" | custom-call | tf_op jit(solution)/shard_map/prepare/pallas_call | solution.py:203
  19.5 0.0 copy-start.2
  19.5 0.0 copy-start.3
  19.5 0.0 copy-start.4
  19.5 0.0 copy-start.5
  19.5 0.0 copy-start.7
  19.5 0.0 copy-start.8
  19.5 10.0 %attention.1 = (bf16[512,256]{1,0:T(8,128)(2,1)S(1)}, bf16[256,512]{1,0:T(8,128)(2,1)S(1)}, f32[144,256]{1,0:T(8,128)S(1)}, f32[144,128]{1,0:T(8,128)S(1)}) custom-call(s32[4,2]{1,0:T(4,128)S(1)} %get-tuple-element.40.spans, bf16[256,512]{1,0:T(8,128)(2,1)S(1)} %get-tuple-element.42.qt_ref, bf16[128,512]{1,0:T(8,128)(2,1)S(1)} %get-tuple-element.43.f_ref, ...), custom_call_target="tpu_custom_call" | custom-call | tf_op jit(solution)/shard_map/attention/pallas_call | solution.py:357
  29.5 0.0 copy-done.2
  29.5 0.0 copy-done.3
  29.5 0.0 copy-done.4
  29.6 0.0 copy-done.5
  29.6 0.0 copy-done.7
  29.6 0.0 copy-done.8
  29.6 13.4 %pooling.1 = (f32[512,256]{1,0:T(8,128)S(1)}, bf16[512,256]{1,0:T(8,128)(2,1)S(1)}, bf16[256,512]{1,0:T(8,128)(2,1)S(1)}, bf16[256,512]{1,0:T(8,128)(2,1)S(1)}, ...) custom-call(f32[144,256]{1,0:T(8,128)S(1)} %get-tuple-element.47.sums,, ...), custom_call_target="tpu_custom_call" | custom-call | tf_op jit(solution)/shard_map/pooling/pallas_call | solution.py:457
  43.0 0.0 copy-start
  43.0 0.0 copy-start.1
  43.0 0.0 copy-start.6
  43.0 16.4 %attention_back.1 = (bf16[512,256]{1,0:T(8,128)(2,1)S(1)}, bf16[1536,256]{1,0:T(8,128)(2,1)S(1)}, bf16[1536,256]{1,0:T(8,128)(2,1)S(1)}) custom-call(s32[4,2]{1,0:T(4,128)S(1)} %get-tuple-element.40.spans, bf16[512,256]{1,0:T(8,128)(2,1)S(1)} %get-tuple-element.41.q_ref, bf16[256,512]{1,0:T(8,128)(2,1)S(1)} %get-tuple-element.42.qt_ref, ...), custom_call_target="tpu_custom_call" | custom-call | tf_op jit(solution)/shard_map/attention_back/pallas_call | solution.py:577
  59.4 0.0 copy-done
  59.4 0.0 copy-done.1
  59.4 0.0 copy-done.6
  59.4 37.8 %finish.1 = (f32[512,256]{1,0:T(8,128)S(1)}, bf16[3072,128]{1,0:T(8,128)(2,1)S(1)}, f32[16,128]{1,0:T(8,128)S(1)}) custom-call(bf16[1536,256]{1,0:T(8,128)(2,1)S(1)} %get-tuple-element.39.hidden, bf16[512,256]{1,0:T(8,128)(2,1)S(1)} %get-tuple-element.53.dq, bf16[1536,256]{1,0:T(8,128)(2,1)S(1)} %get-tuple-element.54.dk, ...), custom_call_target="tpu_custom_call" | custom-call | tf_op jit(solution)/shard_map/finish/pallas_call | solution.py:775
  97.2 1.9 %unpack.1 = (f32[256,768]{1,0:T(8,128)}, f32[256,256]{1,0:T(8,128)}, f32[1,256]{1,0:T(1,128)}, f32[256,512]{1,0:T(8,128)}, f32[1,512]{1,0:T(1,128)}, /*index=5*/f32[1,512]{1,0:T(1,128)}, f32[512,256]{1,0:T(8,128)}) custom-call(bf16[3072,128]{1,0:T(8,128)(2,1)S(1)} %get-tuple-element.61.reduced, f32[16,128]{1,0:T(8,128)S(1)} %get-tuple-element.62.extras, ...), custom_call_target="tpu_custom_call" | custom-call | tf_op jit(solution)/shard_map/unpack/pallas_call | solution.py:828
Async XLA Ops:
  19.5 10.1 %copy-start.2 = (bf16[256,256]{1,0:T(8,128)(2,1)S(1)}, bf16[256,256]{1,0:T(8,128)(2,1)}, u32[]{:S(2)}) copy-start(bf16[256,256]{1,0:T(8,128)(2,1)} %w_out.1) | copy-start | bytes 393220
  19.5 10.1 %copy-start.3 = (bf16[256,512]{1,0:T(8,128)(2,1)S(1)}, bf16[256,512]{1,0:T(8,128)(2,1)}, u32[]{:S(2)}) copy-start(bf16[256,512]{1,0:T(8,128)(2,1)} %w_pool.1) | copy-start | bytes 786436
  19.5 10.1 %copy-start.4 = (f32[128,512]{1,0:T(8,128)S(1)}, f32[128,512]{1,0:T(8,128)}, u32[]{:S(2)}) copy-start(f32[128,512]{1,0:T(8,128)} %cotangent.1) | copy-start | bytes 786436
  19.5 10.1 %copy-start.5 = (s32[512]{0:T(512)S(1)}, s32[512]{0:T(512)}, u32[]{:S(2)}) copy-start(s32[512]{0:T(512)} %param.12) | copy-start | bytes 6148
  19.5 10.1 %copy-start.7 = (f32[512]{0:T(512)S(1)}, f32[512]{0:T(512)}, u32[]{:S(2)}) copy-start(f32[512]{0:T(512)} %param.17) | copy-start | bytes 6148
  19.5 10.1 %copy-start.8 = (f32[512]{0:T(512)S(1)}, f32[512]{0:T(512)}, u32[]{:S(2)}) copy-start(f32[512]{0:T(512)} %param.18) | copy-start | bytes 6148
  43.0 16.4 %copy-start = (bf16[512,256]{1,0:T(8,128)(2,1)S(1)}, bf16[512,256]{1,0:T(8,128)(2,1)}, u32[]{:S(2)}) copy-start(bf16[512,256]{1,0:T(8,128)(2,1)} %points.1) | copy-start | bytes 786436
  43.0 16.4 %copy-start.1 = (bf16[256,768]{1,0:T(8,128)(2,1)S(1)}, bf16[256,768]{1,0:T(8,128)(2,1)}, u32[]{:S(2)}) copy-start(bf16[256,768]{1,0:T(8,128)(2,1)} %w_qkv.1) | copy-start | bytes 1179652
  43.0 16.4 %copy-start.6 = (f32[256]{0:T(256)S(1)}, f32[256]{0:T(256)}, u32[]{:S(2)}) copy-start(f32[256]{0:T(256)} %param.13) | copy-start | bytes 3076

commit v4 on v3

--- a/solution.py
+++ b/solution.py
@@ -125,26 +125,31 @@
     local[0].wait()
     marks[:4, :] = ids[...] + 1
     local[1].wait()
-    copies = [
-        send(points, rows_high, sems, 0, before),
-        send(points, rows_low, sems, 1, after),
-        send(marks, marks_high, sems, 2, before),
-        send(marks, marks_low, sems, 3, after),
-    ]
+    copies = [send(marks, marks_high, sems, 0, before), send(marks, marks_low, sems, 1, after)]
+    parts = [pl.ds(i * TILE * 2, TILE * 2) for i in range(2)]
+    halo = []
+    for i, part in enumerate(parts):
+        halo.append(
+            (
+                send(points.at[part], rows_high.at[part], sems, 2 + 2 * i, before),
+                send(points.at[part], rows_low.at[part], sems, 3 + 2 * i, after),
+            )
+        )
     local[2].wait()
     local[3].wait()
 
     def project(block, first, columns):
-        normed, _ = layer_stats(block[...].astype(jnp.float32))
+        normed, _ = layer_stats(block.astype(jnp.float32))
         hidden = (normed * gain[...]).astype(jnp.bfloat16)
-        hidden_ref[first : first + PATCH, :] = hidden
+        hidden_ref[first : first + block.shape[0], :] = hidden
         return jnp.dot(hidden, w_qkv[:, columns], preferred_element_type=jnp.float32)
 
     def place(first, keys, values):
         for g in range(2):
             lanes = slice(g * HALF, (g + 1) * HALF)
-            kg_ref[g, first : first + PATCH, :HALF] = keys[:, lanes].astype(jnp.bfloat16)
-            vg_ref[g, first : first + PATCH, :HALF] = values[:, lanes].astype(jnp.bfloat16)
+            rows = slice(first, first + keys.shape[0])
+            kg_ref[g, rows, :HALF] = keys[:, lanes].astype(jnp.bfloat16)
+            vg_ref[g, rows, :HALF] = values[:, lanes].astype(jnp.bfloat16)
 
     def place_marks(block, first, own):
         lane = lax.broadcasted_iota(jnp.int32, (HALF, HALF), 1)
@@ -161,7 +166,7 @@
                 away = jnp.where(row < LOG_LANE, (1.0 - digits) * -FAR, 0.0)
                 f_ref[:, i * HALF : (i + 1) * HALF] = away.astype(jnp.bfloat16)
 
-    qkv = project(points, PATCH, slice(None))
+    qkv = project(points[...], PATCH, slice(None))
     queries = qkv[:, :256].astype(jnp.bfloat16).astype(jnp.float32) * 0.25
     q_ref[...] = queries.astype(jnp.bfloat16)
     qt_ref[...] = queries.T.astype(jnp.bfloat16)
@@ -173,7 +178,7 @@
     for g in range(2):
         kg_ref[g, WINDOW:, :] = nowhere
         vg_ref[g, WINDOW:, :] = nowhere
-    for copy in copies[2:]:
+    for copy in copies:
         copy.wait()
     low = jnp.where(me == 0, 0, marks_low[...])
     high = jnp.where(me == lax.axis_size("pts") - 1, 0, marks_high[...])
@@ -191,10 +196,11 @@
         count = (PATCH + upper.astype(jnp.int32) - lower + CHUNK - 1) // CHUNK
         spans_ref[t, 0] = jnp.minimum(lower, TALL - count * CHUNK)
         spans_ref[t, 1] = count
-    for copy, block, first in ((copies[1], rows_low, 0), (copies[0], rows_high, 2 * PATCH)):
-        copy.wait()
-        kv = project(block, first, slice(256, 768))
-        place(first, kv[:, :256], kv[:, 256:])
+    for part, (high_copy, low_copy) in zip(parts, halo):
+        for copy, block, first in ((low_copy, rows_low, 0), (high_copy, rows_high, 2 * PATCH)):
+            copy.wait()
+            kv = project(block[part, :], first + part.start, slice(256, 768))
+            place(first + part.start, kv[:, :256], kv[:, 256:])
 
 
 def prepare(points, ids, gain, w_qkv):
@@ -223,7 +229,7 @@
             pltpu.VMEM((8, HALF), jnp.int32),
             pltpu.VMEM((PATCH, 256), half),
             pltpu.VMEM((PATCH, 256), half),
-            pltpu.SemaphoreType.DMA((2, 4)),
+            pltpu.SemaphoreType.DMA((2, 6)),
             pltpu.SemaphoreType.DMA((4,)),
         ],
         compiler_params=pltpu.CompilerParams(
@@ -397,6 +403,21 @@
         send(ahead_pack, from_before, sems, 1, after),
     ]
     member = membership(cells[...]).astype(jnp.bfloat16)
+    early_rows = HALF - 16
+
+    def cells_back(sums, counts, cotangent):
+        pooled_mean = (sums / counts).astype(jnp.bfloat16)
+        pre_norm = jnp.dot(pooled_mean, w_pool[...], preferred_element_type=jnp.float32) + b_pool[...]
+        pooled_normed, pooled_inv = layer_stats(pre_norm)
+        slope_grad = cotangent * gelu_slope(pooled_normed * pool_gain[...])
+        grad_pre = norm_back(slope_grad * pool_gain[...], pooled_normed, pooled_inv)
+        grad_pre_b = grad_pre.astype(jnp.bfloat16)
+        share = against_rows(grad_pre_b, w_pool[...]) / counts
+        return pooled_mean, pooled_normed, slope_grad, grad_pre, grad_pre_b, share
+
+    early_back = cells_back(
+        sums[:early_rows, :], counts[:early_rows, :1], cotangent[:early_rows, :]
+    )
     for copy in copies:
         copy.wait()
     row = lax.broadcasted_iota(jnp.int32, (8, 1), 0)
@@ -406,21 +427,19 @@
     last_count = counts[HALF - 8 : HALF, :] + jnp.where(row == 7, late[:, 256:], 0.0)
     lead_count = jnp.where(row == 0, counts[HALF : HALF + 8, :] + early[:, 256:384], 0.0)
     spare = jnp.zeros((8, 256), jnp.float32)
-    all_sums = jnp.concatenate([sums[: HALF - 8, :], last_sum, lead_sum, spare], axis=0)
-    all_counts = jnp.concatenate(
-        [counts[: HALF - 8, :], last_count, lead_count, spare[:, :HALF]], axis=0
+    middle = slice(early_rows, HALF - 8)
+    late_sums = jnp.concatenate([sums[middle, :], last_sum, lead_sum, spare], axis=0)
+    late_counts = jnp.concatenate(
+        [counts[middle, :], last_count, lead_count, spare[:, :HALF]], axis=0
     )[:, :1]
-    all_counts = jnp.maximum(all_counts, 1.0)
     lead_cot = jnp.where(row == 0, early[:, 384:], 0.0)
-    all_cot = jnp.concatenate([cotangent[...], lead_cot, jnp.zeros((8, 512), jnp.float32)], axis=0)
-
-    pooled_mean = (all_sums / all_counts).astype(jnp.bfloat16)
-    pre_norm = jnp.dot(pooled_mean, w_pool[...], preferred_element_type=jnp.float32) + b_pool[...]
-    pooled_normed, pooled_inv = layer_stats(pre_norm)
-    slope_grad = all_cot * gelu_slope(pooled_normed * pool_gain[...])
-    grad_pre = norm_back(slope_grad * pool_gain[...], pooled_normed, pooled_inv)
-    grad_pre_b = grad_pre.astype(jnp.bfloat16)
-    share = against_rows(grad_pre_b, w_pool[...]) / all_counts
+    late_cot = jnp.concatenate(
+        [cotangent[early_rows:, :], lead_cot, jnp.zeros((8, 512), jnp.float32)], axis=0
+    )
+    late_back = cells_back(late_sums, jnp.maximum(late_counts, 1.0), late_cot)
+    pooled_mean, pooled_normed, slope_grad, grad_pre, grad_pre_b, share = (
+        jnp.concatenate(pair, axis=0) for pair in zip(early_back, late_back)
+    )
     share_b = share.astype(jnp.bfloat16)
     rest_b = (share - share_b.astype(jnp.float32)).astype(jnp.bfloat16)
     dmixed_main = inner_rows(member, share_b)
@@ -690,12 +709,6 @@
     core_copies = [
         send(send_c.at[1 - core, q], recv_c.at[q], sems, k, core_device) for k, q in enumerate(quarters)
     ]
-    rims = [
-        send(dk.at[pl.ds(0, PATCH)], high_k, sems, 60, before),
-        send(dv.at[pl.ds(0, PATCH)], high_v, sems, 61, before),
-        send(dk.at[pl.ds(2 * PATCH, PATCH)], low_k, sems, 62, after),
-        send(dv.at[pl.ds(2 * PATCH, PATCH)], low_v, sems, 63, after),
-    ]
     extra_copy.wait()
     extra = (extra_own[...].astype(jnp.float32) + extra_in[...].astype(jnp.float32)).astype(jnp.bfloat16)
     copies = []
@@ -709,6 +722,12 @@
         else:
             recv_x[x, :X_ROWS, :] = total.astype(jnp.bfloat16)
             recv_x[x, X_ROWS:, :] = extra
+    rims = [
+        send(dk.at[pl.ds(0, PATCH)], high_k, sems, 60, before),
+        send(dv.at[pl.ds(0, PATCH)], high_v, sems, 61, before),
+        send(dk.at[pl.ds(2 * PATCH, PATCH)], low_k, sems, 62, after),
+        send(dv.at[pl.ds(2 * PATCH, PATCH)], low_v, sems, 63, after),
+    ]
     dhidden = against_rows(dq[...], w_qkv[:, :256])
     normed, inv_std = layer_stats(points[...].astype(jnp.float32))
     wait_all(copies)

time: 99.3 us -> 99.3 us (level)
    pallas_call x1, Pallas kernels: 13.4 us -> 10.1 us  [pool(): pl.pallas_call(functools.partial(pool_kernel, scale), out_shape=[jax.Shap...]
    pallas_call x1, Pallas kernels: 37.8 us -> 40.4 us  [finish(): pl.pallas_call(functools.partial(finish_kernel, scale), out_shape=[jax.Sh...]
where the time goes in v4:
time: 99.3 us; the launch traced here: 98.8 us
  Pallas kernels  97.9 us (99%)
    pallas_call x1, Pallas kernels, finish(): pl.pallas_call(functools.partial(finish_kernel, scale), out_shape=[jax.Sh...  40.4 us
    pallas_call x1, Pallas kernels, prepare(): pl.pallas_call(prepare_kernel, out_shape=[jax.ShapeDtypeStruct((PATCH, 25...  19.2 us
    pallas_call x1, Pallas kernels, attend_back(): pl.pallas_call(backward_kernel, out_shape=[jax.ShapeDtypeStruct((PATCH, 2...  16.4 us
    pallas_call x1, Pallas kernels, pool(): pl.pallas_call(functools.partial(pool_kernel, scale), out_shape=[jax.Shap...  10.1 us
    pallas_call x1, Pallas kernels, attend(): pl.pallas_call(forward_kernel, out_shape=[jax.ShapeDtypeStruct((PATCH, 25...  9.96 us

profile of v4, /device:TPU:1, one launch (start us, length us, event | category | flops | bytes accessed | tf_op | source)
XLA Modules:
  0.0 98.8 jit_solution(1003130100470028106)
XLA Ops:
  0.6 19.2 %prepare.1 = (bf16[512,256]{1,0:T(8,128)(2,1)S(1)}, bf16[256,512]{1,0:T(8,128)(2,1)S(1)}, bf16[2,1584,256]{2,1,0:T(8,128)(2,1)S(1)}, bf16[2,1584,256]{2,1,0:T(8,...) custom-call(bf16[512,256]{1,0:T(8,128)(2,1)} %points.1, ...), custom_call_target="tpu_custom_call" | custom-call | tf_op jit(solution)/shard_map/prepare/pallas_call | solution.py:209
  19.9 0.0 copy-start.2
  19.9 0.0 copy-start.3
  19.9 0.0 copy-start.4
  19.9 0.0 copy-start.5
  19.9 0.0 copy-start.7
  19.9 0.0 copy-start.8
  19.9 10.0 %attention.1 = (bf16[512,256]{1,0:T(8,128)(2,1)S(1)}, bf16[256,512]{1,0:T(8,128)(2,1)S(1)}, f32[144,256]{1,0:T(8,128)S(1)}, f32[144,128]{1,0:T(8,128)S(1)}) custom-call(s32[4,2]{1,0:T(4,128)S(1)} %get-tuple-element.40.spans, bf16[256,512]{1,0:T(8,128)(2,1)S(1)} %get-tuple-element.42.qt_ref, bf16[128,512]{1,0:T(8,128)(2,1)S(1)} %get-tuple-element.43.f_ref, ...), custom_call_target="tpu_custom_call" | custom-call | tf_op jit(solution)/shard_map/attention/pallas_call | solution.py:363
  29.9 0.0 copy-done.2
  29.9 0.0 copy-done.3
  29.9 0.0 copy-done.4
  29.9 0.0 copy-done.5
  29.9 0.0 copy-done.7
  29.9 0.0 copy-done.8
  30.0 10.1 %pooling.1 = (f32[512,256]{1,0:T(8,128)S(1)}, bf16[512,256]{1,0:T(8,128)(2,1)S(1)}, bf16[256,512]{1,0:T(8,128)(2,1)S(1)}, bf16[256,512]{1,0:T(8,128)(2,1)S(1)}, ...) custom-call(f32[144,256]{1,0:T(8,128)S(1)} %get-tuple-element.47.sums,, ...), custom_call_target="tpu_custom_call" | custom-call | tf_op jit(solution)/shard_map/pooling/pallas_call | solution.py:476
  40.1 0.0 copy-start
  40.1 0.0 copy-start.1
  40.1 0.0 copy-start.6
  40.1 16.4 %attention_back.1 = (bf16[512,256]{1,0:T(8,128)(2,1)S(1)}, bf16[1536,256]{1,0:T(8,128)(2,1)S(1)}, bf16[1536,256]{1,0:T(8,128)(2,1)S(1)}) custom-call(s32[4,2]{1,0:T(4,128)S(1)} %get-tuple-element.40.spans, bf16[512,256]{1,0:T(8,128)(2,1)S(1)} %get-tuple-element.41.q_ref, bf16[256,512]{1,0:T(8,128)(2,1)S(1)} %get-tuple-element.42.qt_ref, ...), custom_call_target="tpu_custom_call" | custom-call | tf_op jit(solution)/shard_map/attention_back/pallas_call | solution.py:596
  56.5 0.0 copy-done
  56.5 0.0 copy-done.1
  56.5 0.0 copy-done.6
  56.5 40.4 %finish.1 = (f32[512,256]{1,0:T(8,128)S(1)}, bf16[3072,128]{1,0:T(8,128)(2,1)S(1)}, f32[16,128]{1,0:T(8,128)S(1)}) custom-call(bf16[1536,256]{1,0:T(8,128)(2,1)S(1)} %get-tuple-element.39.hidden, bf16[512,256]{1,0:T(8,128)(2,1)S(1)} %get-tuple-element.53.dq, bf16[1536,256]{1,0:T(8,128)(2,1)S(1)} %get-tuple-element.54.dk, ...), custom_call_target="tpu_custom_call" | custom-call | tf_op jit(solution)/shard_map/finish/pallas_call | solution.py:794
  96.9 1.9 %unpack.1 = (f32[256,768]{1,0:T(8,128)}, f32[256,256]{1,0:T(8,128)}, f32[1,256]{1,0:T(1,128)}, f32[256,512]{1,0:T(8,128)}, f32[1,512]{1,0:T(1,128)}, /*index=5*/f32[1,512]{1,0:T(1,128)}, f32[512,256]{1,0:T(8,128)}) custom-call(bf16[3072,128]{1,0:T(8,128)(2,1)S(1)} %get-tuple-element.61.reduced, f32[16,128]{1,0:T(8,128)S(1)} %get-tuple-element.62.extras, ...), custom_call_target="tpu_custom_call" | custom-call | tf_op jit(solution)/shard_map/unpack/pallas_call | solution.py:847
Async XLA Ops:
  19.9 10.0 %copy-start.2 = (bf16[256,256]{1,0:T(8,128)(2,1)S(1)}, bf16[256,256]{1,0:T(8,128)(2,1)}, u32[]{:S(2)}) copy-start(bf16[256,256]{1,0:T(8,128)(2,1)} %w_out.1) | copy-start | bytes 393220
  19.9 10.0 %copy-start.3 = (bf16[256,512]{1,0:T(8,128)(2,1)S(1)}, bf16[256,512]{1,0:T(8,128)(2,1)}, u32[]{:S(2)}) copy-start(bf16[256,512]{1,0:T(8,128)(2,1)} %w_pool.1) | copy-start | bytes 786436
  19.9 10.0 %copy-start.4 = (f32[128,512]{1,0:T(8,128)S(1)}, f32[128,512]{1,0:T(8,128)}, u32[]{:S(2)}) copy-start(f32[128,512]{1,0:T(8,128)} %cotangent.1) | copy-start | bytes 786436
  19.9 10.0 %copy-start.5 = (s32[512]{0:T(512)S(1)}, s32[512]{0:T(512)}, u32[]{:S(2)}) copy-start(s32[512]{0:T(512)} %param.12) | copy-start | bytes 6148
  19.9 10.0 %copy-start.7 = (f32[512]{0:T(512)S(1)}, f32[512]{0:T(512)}, u32[]{:S(2)}) copy-start(f32[512]{0:T(512)} %param.17) | copy-start | bytes 6148
  19.9 10.0 %copy-start.8 = (f32[512]{0:T(512)S(1)}, f32[512]{0:T(512)}, u32[]{:S(2)}) copy-start(f32[512]{0:T(512)} %param.18) | copy-start | bytes 6148
  40.1 16.4 %copy-start = (bf16[512,256]{1,0:T(8,128)(2,1)S(1)}, bf16[512,256]{1,0:T(8,128)(2,1)}, u32[]{:S(2)}) copy-start(bf16[512,256]{1,0:T(8,128)(2,1)} %points.1) | copy-start | bytes 786436
  40.1 16.4 %copy-start.1 = (bf16[256,768]{1,0:T(8,128)(2,1)S(1)}, bf16[256,768]{1,0:T(8,128)(2,1)}, u32[]{:S(2)}) copy-start(bf16[256,768]{1,0:T(8,128)(2,1)} %w_qkv.1) | copy-start | bytes 1179652
  40.1 16.4 %copy-start.6 = (f32[256]{0:T(256)S(1)}, f32[256]{0:T(256)}, u32[]{:S(2)}) copy-start(f32[256]{0:T(256)} %param.13) | copy-start | bytes 3076

commit v5 on v4

--- a/solution.py
+++ b/solution.py
@@ -732,12 +732,20 @@
     normed, inv_std = layer_stats(points[...].astype(jnp.float32))
     wait_all(copies)
     extra = slot_sum(recv_x, X_ROWS, EXTRA).astype(jnp.bfloat16)
-    for r in range(8):
-        send_y[r, :Y_ROWS, :] = slot_sum(recv_x, r * Y_ROWS, Y_ROWS).astype(jnp.bfloat16)
-        send_y[r, Y_ROWS:, :] = extra
-
-    copies = swap(on_y, lambda r: send_y.at[r], lambda r: recv_y.at[r], sems, 8)
-    recv_y[on_y[0]] = send_y[on_y[0]]
+    y, y_device = on_y[0], on_y[2]
+    copies = []
+    for k in far_first(8) + [0]:
+        r = (y + k) % 8
+        rows = pl.ds(pl.multiple_of(r * Y_ROWS, Y_ROWS), Y_ROWS)
+        piece = recv_x[0, rows, :].astype(jnp.float32)
+        for q in range(1, 4):
+            piece = piece + recv_x[q, rows, :].astype(jnp.float32)
+        target = send_y.at[r] if k else recv_y.at[y]
+        target[:Y_ROWS, :] = piece.astype(jnp.bfloat16)
+        target[Y_ROWS:, :] = extra
+        if k:
+            copies.append(send(target, recv_y.at[y], sems, 7 + k, y_device(r)))
+    copies = copies[::-1]
     wait_all(rims)
     for columns, mine, low, high in (
         (slice(256, 512), dk, low_k, high_k), (slice(512, 768), dv, low_v, high_v)
@@ -752,7 +760,6 @@
     wait_all(swap(on_z, lambda r: recv_z.at[on_z[0]], lambda r: recv_z.at[r], sems, 15))
     total = slot_sum(recv_z, 0, Y_ROWS + EXTRA)
     extras[...] = total[Y_ROWS:]
-    y, y_device = on_y[0], on_y[2]
     gather_c[core, x, y] = total[:Y_ROWS].astype(jnp.bfloat16)
     order = (1, 7, 2, 6, 3, 5, 4)
 

time: 99.3 us -> 99 us (level)
    pallas_call x1, Pallas kernels: 10.1 us -> 11.7 us  [pool(): pl.pallas_call(functools.partial(pool_kernel, scale), out_shape=[jax.Shap...]
    pallas_call x1, Pallas kernels: 40.4 us -> 39.3 us  [finish(): pl.pallas_call(functools.partial(finish_kernel, scale), out_shape=[jax.Sh...]
where the time goes in v5:
time: 99 us; the launch traced here: 99.4 us
  Pallas kernels  98.5 us (99%)
    pallas_call x1, Pallas kernels, finish(): pl.pallas_call(functools.partial(finish_kernel, scale), out_shape=[jax.Sh...  39.3 us
    pallas_call x1, Pallas kernels, prepare(): pl.pallas_call(prepare_kernel, out_shape=[jax.ShapeDtypeStruct((PATCH, 25...  19.2 us
    pallas_call x1, Pallas kernels, attend_back(): pl.pallas_call(backward_kernel, out_shape=[jax.ShapeDtypeStruct((PATCH, 2...  16.3 us
    pallas_call x1, Pallas kernels, pool(): pl.pallas_call(functools.partial(pool_kernel, scale), out_shape=[jax.Shap...  11.7 us
    pallas_call x1, Pallas kernels, attend(): pl.pallas_call(forward_kernel, out_shape=[jax.ShapeDtypeStruct((PATCH, 25...  9.98 us

profile of v5, /device:TPU:1, one launch (start us, length us, event | category | flops | bytes accessed | tf_op | source)
XLA Modules:
  0.0 99.4 jit_solution(8488931674385356085)
XLA Ops:
  0.6 19.2 %prepare.1 = (bf16[512,256]{1,0:T(8,128)(2,1)S(1)}, bf16[256,512]{1,0:T(8,128)(2,1)S(1)}, bf16[2,1584,256]{2,1,0:T(8,128)(2,1)S(1)}, bf16[2,1584,256]{2,1,0:T(8,...) custom-call(bf16[512,256]{1,0:T(8,128)(2,1)} %points.1, ...), custom_call_target="tpu_custom_call" | custom-call | tf_op jit(solution)/shard_map/prepare/pallas_call | solution.py:209
  19.9 0.0 copy-start.2
  19.9 0.0 copy-start.3
  19.9 0.0 copy-start.4
  19.9 0.0 copy-start.5
  19.9 0.0 copy-start.7
  19.9 0.0 copy-start.8
  19.9 10.0 %attention.1 = (bf16[512,256]{1,0:T(8,128)(2,1)S(1)}, bf16[256,512]{1,0:T(8,128)(2,1)S(1)}, f32[144,256]{1,0:T(8,128)S(1)}, f32[144,128]{1,0:T(8,128)S(1)}) custom-call(s32[4,2]{1,0:T(4,128)S(1)} %get-tuple-element.40.spans, bf16[256,512]{1,0:T(8,128)(2,1)S(1)} %get-tuple-element.42.qt_ref, bf16[128,512]{1,0:T(8,128)(2,1)S(1)} %get-tuple-element.43.f_ref, ...), custom_call_target="tpu_custom_call" | custom-call | tf_op jit(solution)/shard_map/attention/pallas_call | solution.py:363
  29.9 0.0 copy-done.2
  29.9 0.0 copy-done.3
  29.9 0.0 copy-done.4
  29.9 0.0 copy-done.5
  30.0 0.0 copy-done.7
  30.0 0.0 copy-done.8
  30.0 11.7 %pooling.1 = (f32[512,256]{1,0:T(8,128)S(1)}, bf16[512,256]{1,0:T(8,128)(2,1)S(1)}, bf16[256,512]{1,0:T(8,128)(2,1)S(1)}, bf16[256,512]{1,0:T(8,128)(2,1)S(1)}, ...) custom-call(f32[144,256]{1,0:T(8,128)S(1)} %get-tuple-element.47.sums,, ...), custom_call_target="tpu_custom_call" | custom-call | tf_op jit(solution)/shard_map/pooling/pallas_call | solution.py:476
  41.7 0.0 copy-start
  41.7 0.0 copy-start.1
  41.7 0.0 copy-start.6
  41.8 16.3 %attention_back.1 = (bf16[512,256]{1,0:T(8,128)(2,1)S(1)}, bf16[1536,256]{1,0:T(8,128)(2,1)S(1)}, bf16[1536,256]{1,0:T(8,128)(2,1)S(1)}) custom-call(s32[4,2]{1,0:T(4,128)S(1)} %get-tuple-element.40.spans, bf16[512,256]{1,0:T(8,128)(2,1)S(1)} %get-tuple-element.41.q_ref, bf16[256,512]{1,0:T(8,128)(2,1)S(1)} %get-tuple-element.42.qt_ref, ...), custom_call_target="tpu_custom_call" | custom-call | tf_op jit(solution)/shard_map/attention_back/pallas_call | solution.py:596
  58.1 0.0 copy-done
  58.1 0.0 copy-done.1
  58.1 0.0 copy-done.6
  58.1 39.3 %finish.1 = (f32[512,256]{1,0:T(8,128)S(1)}, bf16[3072,128]{1,0:T(8,128)(2,1)S(1)}, f32[16,128]{1,0:T(8,128)S(1)}) custom-call(bf16[1536,256]{1,0:T(8,128)(2,1)S(1)} %get-tuple-element.39.hidden, bf16[512,256]{1,0:T(8,128)(2,1)S(1)} %get-tuple-element.53.dq, bf16[1536,256]{1,0:T(8,128)(2,1)S(1)} %get-tuple-element.54.dk, ...), custom_call_target="tpu_custom_call" | custom-call | tf_op jit(solution)/shard_map/finish/pallas_call | solution.py:801
  97.4 1.9 %unpack.1 = (f32[256,768]{1,0:T(8,128)}, f32[256,256]{1,0:T(8,128)}, f32[1,256]{1,0:T(1,128)}, f32[256,512]{1,0:T(8,128)}, f32[1,512]{1,0:T(1,128)}, /*index=5*/f32[1,512]{1,0:T(1,128)}, f32[512,256]{1,0:T(8,128)}) custom-call(bf16[3072,128]{1,0:T(8,128)(2,1)S(1)} %get-tuple-element.61.reduced, f32[16,128]{1,0:T(8,128)S(1)} %get-tuple-element.62.extras, ...), custom_call_target="tpu_custom_call" | custom-call | tf_op jit(solution)/shard_map/unpack/pallas_call | solution.py:854
Async XLA Ops:
  19.9 10.1 %copy-start.2 = (bf16[256,256]{1,0:T(8,128)(2,1)S(1)}, bf16[256,256]{1,0:T(8,128)(2,1)}, u32[]{:S(2)}) copy-start(bf16[256,256]{1,0:T(8,128)(2,1)} %w_out.1) | copy-start | bytes 393220
  19.9 10.1 %copy-start.3 = (bf16[256,512]{1,0:T(8,128)(2,1)S(1)}, bf16[256,512]{1,0:T(8,128)(2,1)}, u32[]{:S(2)}) copy-start(bf16[256,512]{1,0:T(8,128)(2,1)} %w_pool.1) | copy-start | bytes 786436
  19.9 10.1 %copy-start.4 = (f32[128,512]{1,0:T(8,128)S(1)}, f32[128,512]{1,0:T(8,128)}, u32[]{:S(2)}) copy-start(f32[128,512]{1,0:T(8,128)} %cotangent.1) | copy-start | bytes 786436
  19.9 10.1 %copy-start.5 = (s32[512]{0:T(512)S(1)}, s32[512]{0:T(512)}, u32[]{:S(2)}) copy-start(s32[512]{0:T(512)} %param.12) | copy-start | bytes 6148
  19.9 10.1 %copy-start.7 = (f32[512]{0:T(512)S(1)}, f32[512]{0:T(512)}, u32[]{:S(2)}) copy-start(f32[512]{0:T(512)} %param.17) | copy-start | bytes 6148
  19.9 10.1 %copy-start.8 = (f32[512]{0:T(512)S(1)}, f32[512]{0:T(512)}, u32[]{:S(2)}) copy-start(f32[512]{0:T(512)} %param.18) | copy-start | bytes 6148
  41.7 16.4 %copy-start = (bf16[512,256]{1,0:T(8,128)(2,1)S(1)}, bf16[512,256]{1,0:T(8,128)(2,1)}, u32[]{:S(2)}) copy-start(bf16[512,256]{1,0:T(8,128)(2,1)} %points.1) | copy-start | bytes 786436
  41.7 16.4 %copy-start.1 = (bf16[256,768]{1,0:T(8,128)(2,1)S(1)}, bf16[256,768]{1,0:T(8,128)(2,1)}, u32[]{:S(2)}) copy-start(bf16[256,768]{1,0:T(8,128)(2,1)} %w_qkv.1) | copy-start | bytes 1179652
  41.7 16.4 %copy-start.6 = (f32[256]{0:T(256)S(1)}, f32[256]{0:T(256)}, u32[]{:S(2)}) copy-start(f32[256]{0:T(256)} %param.13) | copy-start | bytes 3076
